TPU v7x, 128 devices: a whole 4x4x4 slice. The times are simulated.
128 devices in a mesh: dom: 128 (over y, z, x, core).
Axes of the slice: x: 4, y: 4, z: 4, core: 2. Of those that a mesh axis runs over, the one named last changes fastest.
Arguments:
- features: bfloat16 [524288, 128], P('dom'), may hold values from -6 to 6
- cotangent: bfloat16 [524288, 128], P('dom'), may hold values from -6 to 6
- weights: bfloat16 [4, 128, 128], replicated, may hold values from -0.5 to 0.5
- fine_tiles: bfloat16 [4096, 12, 128, 128], P('dom'), may hold values from -0.15625 to 0.15625
- fine_columns: int32 [128, 32, 12], P('dom'), may hold values from 0 to 39, as said below
- fine_halo: int32 [128, 4, 256], P('dom'), may hold values from 0 to 4095
- coarse_tiles: bfloat16 [2560, 12, 128, 128], P('dom'), may hold values from -0.15625 to 0.15625
- coarse_columns: int32 [128, 20, 12], P('dom'), may hold values from 0 to 27, as said below
- coarse_halo: int32 [128, 4, 256], P('dom'), may hold values from 0 to 2559, as said below
- pair_send: int32 [128, 4, 256], P('dom'), may hold values from 0 to 4095, as said below
- members: int32 [128, 2, 2560], P('dom'), may hold values from 0 to 5119, as said below
- coarse_count: int32 [128], P('dom'), may hold values from 1536 to 2560
Outputs:
- result: bfloat16 [524288, 128], P('dom')
- grad_features: bfloat16 [524288, 128], P('dom')
- grad_weights: float32 [4, 128, 128], replicated
Inputs may be any that keep to these rules, and one draw needn't show every extreme that they name: `fine_columns`: entry 0 of row block b is b itself and entry 1 is halo block 32 + (b mod 8). `coarse_columns`: entry 0 of row block b is b itself and entry 1 is halo block 20 + (b mod 8). `coarse_halo`: entries of partition p are below coarse_count[p]; in direction 0 the first entry is coarse_count[p] - 1 and the second is 0. `pair_send`: the 1024 entries of one partition are different rows. `members`: A live cell names two different rows; dead cells name row 0 twice. Every fine row belongs to exactly one live cell, of its own partition or of the neighbour that receives it.
All inputs are finite; a program needn't handle non-finite values.
Results may differ from a plain program's by a relative error of at most 0.013.
Values may be sent and summed in bfloat16 or wider, within the bound.
A program may use at most 192 MiB of HBM per device.

v0:
```python
import jax
import jax.numpy as jnp
from jax import lax
from jax.sharding import PartitionSpec as P

OFFSETS = (1, -1, 8, -8)


def from_behind(block, axis, distance):
    devices = range(lax.axis_size(axis))
    route = [((i - distance) % len(devices), i) for i in devices]
    return lax.ppermute(block, axis, route)


def silu_grad(value):
    sigma = jax.nn.sigmoid(value)
    return sigma * (1.0 + value * (1.0 - sigma))


def project(values, weight):
    return jnp.dot(values, weight, preferred_element_type=jnp.float32).astype(jnp.bfloat16)


def rows_ahead(pieces):
    return [from_behind(pieces[index], "dom", OFFSETS[index]) for index in range(4)]


def rows_behind(pieces):
    return [from_behind(pieces[index], "dom", -OFFSETS[index]) for index in range(4)]


def grads_behind(pieces):
    return [
        from_behind(pieces[index].astype(jnp.bfloat16), "dom", -OFFSETS[index]).astype(jnp.float32)
        for index in range(4)
    ]


def outgoing_rows(values, send_rows, weight):
    own_rows = project(values, weight)
    return (own_rows, [jnp.take(own_rows, send_rows[index], axis=0) for index in range(4)])


def finish(own_rows, arrived):
    return jnp.concatenate([own_rows] + arrived, axis=0)


def aggregate(tile_values, columns, extended):
    tile_size = tile_values.shape[-1]
    feature_width = extended.shape[-1]
    blocks = extended.reshape(-1, tile_size, feature_width)[columns]
    summed = jnp.einsum("bktu,bkuh->bth", tile_values, blocks, preferred_element_type=jnp.float32)
    return summed.reshape(-1, feature_width)


def spread(tile_values, columns, gradient, block_count):
    tile_size = tile_values.shape[-1]
    feature_width = gradient.shape[-1]
    partial_value = jnp.einsum(
        "bktu,bth->bkuh",
        tile_values,
        gradient.reshape(tile_values.shape[0], tile_size, feature_width),
        preferred_element_type=jnp.float32,
    )
    summed_rows = (
        jnp.zeros((block_count, tile_size, feature_width), jnp.float32)
        .at[columns.reshape(-1)]
        .add(partial_value.reshape(-1, tile_size, feature_width))
    )
    return summed_rows.reshape(block_count * tile_size, feature_width)


def retract(grad_ext, send_rows, row_count, halo_rows):
    own_rows = grad_ext[:row_count]
    pieces = [
        grad_ext[row_count + index * halo_rows : row_count + (index + 1) * halo_rows]
        for index in range(4)
    ]
    returned = grads_behind(pieces)
    for index in range(4):
        own_rows = own_rows.at[send_rows[index]].add(returned[index])
    return own_rows


def level_rest(values, extended, update_weight, tile_values, columns):
    summed = aggregate(tile_values, columns, extended)
    gated_rows = jax.nn.silu(summed).astype(jnp.bfloat16)
    output = (
        values.astype(jnp.float32)
        + jnp.dot(gated_rows, update_weight, preferred_element_type=jnp.float32)
    ).astype(jnp.bfloat16)
    return (output, summed, gated_rows)


def level_backward(
    values,
    summed,
    gated_rows,
    grad_out,
    message_weight,
    update_weight,
    tile_values,
    columns,
    send_rows,
):
    row_count = values.shape[0]
    halo_rows = send_rows.shape[1]
    block_count = (row_count + 4 * halo_rows) // tile_values.shape[-1]
    grad_low = grad_out.astype(jnp.bfloat16)
    grad_update = jnp.dot(gated_rows.T, grad_low, preferred_element_type=jnp.float32)
    grad_gated = jnp.dot(grad_low, update_weight.T, preferred_element_type=jnp.float32)
    grad_summed = (grad_gated * silu_grad(summed)).astype(jnp.bfloat16)
    grad_ext = spread(tile_values, columns, grad_summed, block_count)
    grad_msg = retract(grad_ext, send_rows, row_count, halo_rows)
    msg_low = grad_msg.astype(jnp.bfloat16)
    grad_message = jnp.dot(values.T, msg_low, preferred_element_type=jnp.float32)
    grad_values = grad_out + jnp.dot(msg_low, message_weight.T, preferred_element_type=jnp.float32)
    return (grad_values, grad_message, grad_update)


def pool_rows(own_rows, arrived, member_rows, alive_mask):
    extended = jnp.concatenate([own_rows] + arrived, axis=0)
    summed_rows = jnp.take(extended, member_rows[0], axis=0).astype(jnp.float32) + jnp.take(
        extended, member_rows[1], axis=0
    ).astype(jnp.float32)
    return jnp.where(alive_mask[:, None], summed_rows, jnp.float32(0.0))


def unpool_parts(values, member_rows, alive_mask, row_count, pair_count):
    masked = jnp.where(alive_mask[:, None], values, jnp.zeros_like(values))
    extended = jnp.zeros((row_count + 4 * pair_count, values.shape[-1]), values.dtype)
    extended = extended.at[member_rows[0]].add(masked).at[member_rows[1]].add(masked)
    return (
        extended[:row_count],
        [
            extended[row_count + index * pair_count : row_count + (index + 1) * pair_count]
            for index in range(4)
        ],
    )


def per_device(
    features,
    cotangent,
    weights,
    fine_tiles,
    fine_columns,
    fine_halo,
    coarse_tiles,
    coarse_columns,
    coarse_halo,
    pair_send,
    members,
    coarse_count,
):
    fine_send = fine_halo[0]
    coarse_send = coarse_halo[0]
    partner_send = pair_send[0]
    member_rows = members[0]
    row_count = features.shape[0]
    pair_count = partner_send.shape[1]
    alive_mask = jnp.arange(member_rows.shape[1], dtype=jnp.int32) < coarse_count[0]
    cot_rows = [jnp.take(cotangent, partner_send[index], axis=0) for index in range(4)]
    fine_own, fine_outgoing = outgoing_rows(features, fine_send, weights[0])
    fine_arrived = rows_ahead(fine_outgoing)
    fine_ext = finish(fine_own, fine_arrived)
    fine_out, fine_summed, fine_gated = level_rest(
        features, fine_ext, weights[1], fine_tiles, fine_columns[0]
    )
    partner_rows = rows_ahead(
        [jnp.take(fine_out, partner_send[index], axis=0) for index in range(4)]
    )
    coarse_in = pool_rows(fine_out, partner_rows, member_rows, alive_mask).astype(jnp.bfloat16)
    coarse_own, coarse_outgoing = outgoing_rows(coarse_in, coarse_send, weights[2])
    coarse_ext = finish(coarse_own, rows_ahead(coarse_outgoing))
    coarse_out, coarse_summed, coarse_gated = level_rest(
        coarse_in, coarse_ext, weights[3], coarse_tiles, coarse_columns[0]
    )
    own_back, away_rows = unpool_parts(coarse_out, member_rows, alive_mask, row_count, pair_count)
    returned = rows_behind(away_rows)
    lifted = own_back.astype(jnp.float32)
    for index in range(4):
        lifted = lifted.at[partner_send[index]].add(returned[index].astype(jnp.float32))
    result = (fine_out.astype(jnp.float32) + lifted).astype(jnp.bfloat16)
    cot_later = rows_ahead(cot_rows)
    grad_coarse_out = pool_rows(cotangent, cot_later, member_rows, alive_mask)
    grad_coarse_in, grad_two, grad_three = level_backward(
        coarse_in,
        coarse_summed,
        coarse_gated,
        grad_coarse_out,
        weights[2],
        weights[3],
        coarse_tiles,
        coarse_columns[0],
        coarse_send,
    )
    own_grad, away_grad = unpool_parts(
        grad_coarse_in, member_rows, alive_mask, row_count, pair_count
    )
    returned_grad = grads_behind(away_grad)
    grad_fine_out = cotangent.astype(jnp.float32) + own_grad
    for index in range(4):
        grad_fine_out = grad_fine_out.at[partner_send[index]].add(returned_grad[index])
    grad_input, grad_zero, grad_one = level_backward(
        features,
        fine_summed,
        fine_gated,
        grad_fine_out,
        weights[0],
        weights[1],
        fine_tiles,
        fine_columns[0],
        fine_send,
    )
    grad_stack = lax.psum(jnp.stack([grad_zero, grad_one, grad_two, grad_three]), "dom")
    return (result, grad_input.astype(jnp.bfloat16), grad_stack)


def solution(mesh):
    placed = (
        P("dom", None),
        P("dom", None),
        P(),
        P("dom", None, None, None),
        P("dom", None, None),
        P("dom", None, None),
        P("dom", None, None, None),
        P("dom", None, None),
        P("dom", None, None),
        P("dom", None, None),
        P("dom", None, None),
        P("dom"),
    )
    return jax.shard_map(
        per_device,
        mesh=mesh,
        in_specs=placed,
        out_specs=(P("dom", None), P("dom", None), P()),
        check_vma=False,
    )
```

profile of v0, /device:TPU:1, one launch (start us, length us, event | category | flops | bytes accessed | tf_op | source)
XLA Modules:
  0.0 674.7 jit_solution(4100996942695233979)
XLA Ops:
  18.2 5.2 collective-permute-start.3
  44.7 11.3 %gather_fusion = bf16[384,128,128]{2,1,0:T(8,128)(2,1)} fusion(bf16[40,128,128]{2,1,0:T(8,128)(2,1)S(1)} %bitcast.222, s32[1024]{0:T(1024)S(1)} %pad_clamp_fusion.11), kind=kCustom, calls=%fused_computation.20 | custom fusion | bytes 25167360 | tf_op jit(solution)/shard_map/gather | solution.py:51
  56.0 13.0 %fusion.16 = (bf16[32,128,128]{2,1,0:T(8,128)(2,1)S(1)}, f32[32,128,128,1]{1,2,3,0:T(8,128)}) fusion(bf16[32,12,128,128]{3,2,1,0:T(8,128)(2,1)} %param.21, bf16[32,12,128,128]{3,2,1,0:T(8,128)(2,1)} %bitcast.226), kind=kOutput, calls=%fused_computation.75 | convolution fusion | flops 1613234176 | bytes 28311552 | tf_op jit(solution)/shard_map/bktu,bkuh->bth/dot_general | solution.py:52
  85.4 7.2 %collective-permute-start.5 = (bf16[256,128]{1,0:T(8,128)(2,1)S(1)}, bf16[256,128]{1,0:T(8,128)(2,1)S(1)}, u32[]{:S(2)}, u32[]{:S(2)}) collective-permute-start(bf16[256,128]{1,0:T(8,128)(2,1)S(1)} %get-tuple-element.65), channel_id=1, source_target_pairs={{1,0},{2,1},{3,2},{4,3},{5,4},{6,5},{7,6},{8,7},{9,8},{10,9},{11,1... | collective-permute-start | bytes 196616 | tf_op jit(solution)/shard_map/ppermute | solution.py:12
  104.2 6.1 gather_fusion.21
  110.4 6.1 gather_fusion.20
  116.6 5.1 gather_fusion.10
  121.7 5.1 gather_fusion.11
  135.6 5.7 collective-permute-start.11
  142.7 8.4 %gather_fusion.1 = bf16[240,128,128]{2,1,0:T(8,128)(2,1)} fusion(bf16[28,128,128]{2,1,0:T(8,128)(2,1)S(1)} %bitcast.224, s32[1024]{0:T(1024)S(1)} %pad_clamp_fusion.2), kind=kCustom, calls=%fused_computation.21 | custom fusion | bytes 15729600 | tf_op jit(solution)/shard_map/gather | solution.py:51
  151.1 8.8 %fusion.28 = (bf16[20,128,128]{2,1,0:T(8,128)(2,1)S(1)}, f32[20,128,128,1]{1,2,3,0:T(8,128)}) fusion(bf16[20,12,128,128]{3,2,1,0:T(8,128)(2,1)} %param.24, bf16[20,12,128,128]{3,2,1,0:T(8,128)(2,1)} %bitcast.227), kind=kOutput, calls=%fused_computation.94 | convolution fusion | flops 1008271360 | bytes 17694720 | tf_op jit(solution)/shard_map/bktu,bkuh->bth/dot_general | solution.py:52
  161.3 15.7 %scatter_custom_fusion = bf16[5120,128]{1,0:T(8,128)(2,1)S(1)} fusion(s32[2560]{0:T(1024)} %get-tuple-element.13, bf16[2560,128]{1,0:T(8,128)(2,1)S(1)} %fusion.6, bf16[]{:T(256)} %constant.36.clone.1), kind=kCustom, calls=%fused_computation.100 | custom fusion | flops 327680 | bytes 1311232 | tf_op jit(solution)/shard_map/scatter-add | solution.py:132
  177.1 16.2 %scatter_fusion = bf16[5120,128]{1,0:T(8,128)(2,1)S(1)} fusion(bf16[5120,128]{1,0:T(8,128)(2,1)S(1)} %scatter_custom_fusion, s32[2560]{0:T(1024)S(1)} %get-tuple-element.12, bf16[2560,128]{1,0:T(8,128)(2,1)} %copy-done.10), kind=kCustom, calls=%fused_computation.23 | custom fusion | flops 327680 | bytes 1976320 | tf_op jit(solution)/shard_map/scatter-add | solution.py:132
  200.0 11.0 %fusion.98 = f32[20,128,12,128]{3,1,2,0:T(8,128)} fusion(bf16[20,128,128,1]{2,1,3,0:T(8,128)(2,1)S(1)} %bitcast.230, bf16[20,12,128,128]{3,2,1,0:T(8,128)(2,1)} %param.24), kind=kOutput, calls=%fused_computation.270 | convolution fusion | flops 1006632960 | bytes 24248320 | tf_op jit(solution)/shard_map/bktu,bth->bkuh/dot_general | solution.py:59
  211.0 15.6 %copy.25 = f32[240,128,128]{2,1,0:T(8,128)} copy(f32[240,128,128]{1,2,0:T(8,128)} %bitcast.223) | data formatting | bytes 31457280 | tf_op jit(solution)/shard_map/reshape | solution.py:68
  226.8 31.5 %scatter_fusion.1 = f32[28,128,128]{2,1,0:T(8,128)S(1)} fusion(f32[28,128,128]{2,1,0:T(8,128)S(1)} %broadcast_in_dim.70, s32[240]{0:T(256)S(1)} %bitcast.239, f32[240,128,128]{2,1,0:T(8,128)} %copy.25), kind=kCustom, calls=%fused_computation.28 | custom fusion | flops 3932160 | bytes 47186880 | tf_op jit(solution)/shard_map/scatter-add | solution.py:68
  304.8 16.0 %scatter_custom_fusion.11 = f32[5120,128]{1,0:T(8,128)S(1)} fusion(s32[2560]{0:T(1024)} %get-tuple-element.13, f32[2560,128]{1,0:T(8,128)} %fusion.3, f32[]{:T(128)} %constant.38.clone.1), kind=kCustom, calls=%fused_computation.91 | custom fusion | flops 327680 | bytes 2621952 | tf_op jit(solution)/shard_map/scatter-add | solution.py:132
  320.8 16.3 %scatter_fusion.2 = f32[5120,128]{1,0:T(8,128)S(1)} fusion(f32[5120,128]{1,0:T(8,128)S(1)} %scatter_custom_fusion.11, s32[2560]{0:T(1024)S(1)} %get-tuple-element.12, f32[2560,128]{1,0:T(8,128)} %fusion.3), kind=kCustom, calls=%fused_computation.34 | custom fusion | flops 327680 | bytes 3942400 | tf_op jit(solution)/shard_map/scatter-add | solution.py:132
  344.8 8.5 %collective-permute-start.24 = (bf16[256,128]{1,0:T(8,128)(2,1)S(1)}, bf16[256,128]{1,0:T(8,128)(2,1)S(1)}, u32[]{:S(2)}, u32[]{:S(2)}) collective-permute-start(bf16[256,128]{1,0:T(8,128)(2,1)S(1)} %get-tuple-element.27), channel_id=1, source_target_pairs={{1,0},{2,1},{3,2},{4,3},{5,4},{6,5},{7,6},{8,7},{9,8},{10,9},{11,1... | collective-permute-start | bytes 196616 | tf_op jit(solution)/shard_map/ppermute | solution.py:12
  390.7 16.3 %fusion.99 = f32[32,128,12,128]{3,1,2,0:T(8,128)} fusion(bf16[32,128,128,1]{2,1,3,0:T(8,128)(2,1)S(1)} %bitcast.228, bf16[32,12,128,128]{3,2,1,0:T(8,128)(2,1)} %param.21), kind=kOutput, calls=%fused_computation.271 | convolution fusion | flops 1610612736 | bytes 38797312 | tf_op jit(solution)/shard_map/bktu,bth->bkuh/dot_general | solution.py:59
  407.0 24.7 %copy.28 = f32[384,128,128]{2,1,0:T(8,128)} copy(f32[384,128,128]{1,2,0:T(8,128)} %bitcast.221) | data formatting | bytes 50331648 | tf_op jit(solution)/shard_map/reshape | solution.py:68
  432.3 50.2 %scatter_fusion.3 = f32[40,128,128]{2,1,0:T(8,128)S(1)} fusion(f32[40,128,128]{2,1,0:T(8,128)S(1)} %broadcast_in_dim.71, s32[384]{0:T(512)S(1)} %copy-done.29, f32[384,128,128]{2,1,0:T(8,128)} %copy.28), kind=kCustom, calls=%fused_computation.39 | custom fusion | flops 6291456 | bytes 75499008 | tf_op jit(solution)/shard_map/scatter-add | solution.py:68
  485.0 7.9 %collective-permute-start.28 = (bf16[256,128]{1,0:T(8,128)(2,1)S(1)}, bf16[256,128]{1,0:T(8,128)(2,1)S(1)}, u32[]{:S(2)}, u32[]{:S(2)}) collective-permute-start(bf16[256,128]{1,0:T(8,128)(2,1)S(1)} %bitcast.238), channel_id=1, source_target_pairs={{1,0},{2,1},{3,2},{4,3},{5,4},{6,5},{7,6},{8,7},{9,8},{10,9},{11,1... | collective-permute-start | bytes 196616 | tf_op jit(solution)/shard_map/ppermute | solution.py:12
  520.3 145.5 %all-reduce.2.cloned.1.call-done = f32[4,128,128]{1,2,0:T(8,128)} async-done(((f32[4,128,128]{1,2,0:T(8,128)}), f32[4,128,128]{1,2,0:T(8,128)}) %all-reduce.2.cloned.1.call-update) | async-done | bytes 262160 | tf_op jit(solution)/shard_map/psum | solution.py:216
  (286 shorter events, 201.3 us)
Async XLA Ops:
  7.2 658.6 %all-reduce.2.cloned.1.call-start = ((), (), s32[]{:S(2)}) async-start(), calls=%async_computation | async-start | bytes 524288 | tf_op jit(solution)/shard_map/psum | solution.py:216
  10.8 33.8 %collective-permute-start.1 = (bf16[256,128]{1,0:T(8,128)(2,1)S(1)}, bf16[256,128]{1,0:T(8,128)(2,1)S(1)}, u32[]{:S(2)}, u32[]{:S(2)}) collective-permute-start(bf16[256,128]{1,0:T(8,128)(2,1)S(1)} %broadcast_select_fusion.16), channel_id=1, source_target_pairs={{1,0},{2,1},{3,2},{4,3},{5,4},{6,5},{7,6},{8,7},{9,8},{10,9},{11,1... | collective-permute-start | bytes 196616 | tf_op jit(solution)/shard_map/ppermute | solution.py:12
  13.3 31.3 %collective-permute-start = (bf16[256,128]{1,0:T(8,128)(2,1)S(1)}, bf16[256,128]{1,0:T(8,128)(2,1)S(1)}, u32[]{:S(2)}, u32[]{:S(2)}) collective-permute-start(bf16[256,128]{1,0:T(8,128)(2,1)S(1)} %broadcast_select_fusion.17), channel_id=1, source_target_pairs={{127,0},{0,1},{1,2},{2,3},{3,4},{4,5},{5,6},{6,7},{7,8},{8,9},{9,1... | collective-permute-start | bytes 196616 | tf_op jit(solution)/shard_map/ppermute | solution.py:12
  15.5 29.1 %collective-permute-start.2 = (bf16[256,128]{1,0:T(8,128)(2,1)S(1)}, bf16[256,128]{1,0:T(8,128)(2,1)S(1)}, u32[]{:S(2)}, u32[]{:S(2)}) collective-permute-start(bf16[256,128]{1,0:T(8,128)(2,1)S(1)} %broadcast_select_fusion.15), channel_id=1, source_target_pairs={{120,0},{121,1},{122,2},{123,3},{124,4},{125,5},{126,6},{127,7},{0... | collective-permute-start | bytes 196616 | tf_op jit(solution)/shard_map/ppermute | solution.py:12
  18.2 26.5 %collective-permute-start.3 = (bf16[256,128]{1,0:T(8,128)(2,1)S(1)}, bf16[256,128]{1,0:T(8,128)(2,1)S(1)}, u32[]{:S(2)}, u32[]{:S(2)}) collective-permute-start(bf16[256,128]{1,0:T(8,128)(2,1)S(1)} %broadcast_select_fusion.14), channel_id=1, source_target_pairs={{8,0},{9,1},{10,2},{11,3},{12,4},{13,5},{14,6},{15,7},{16,8},{17,9... | collective-permute-start | bytes 196616 | tf_op jit(solution)/shard_map/ppermute | solution.py:12
  78.9 18.8 %collective-permute-start.16 = (bf16[256,128]{1,0:T(8,128)(2,1)S(1)}, bf16[256,128]{1,0:T(8,128)(2,1)S(1)}, u32[]{:S(2)}, u32[]{:S(2)}) collective-permute-start(bf16[256,128]{1,0:T(8,128)(2,1)S(1)} %get-tuple-element.66), channel_id=1, source_target_pairs={{127,0},{0,1},{1,2},{2,3},{3,4},{4,5},{5,6},{6,7},{7,8},{8,9},{9,1... | collective-permute-start | bytes 196616 | tf_op jit(solution)/shard_map/ppermute | solution.py:12
  79.7 36.7 %collective-permute-start.4 = (bf16[256,128]{1,0:T(8,128)(2,1)S(1)}, bf16[256,128]{1,0:T(8,128)(2,1)S(1)}, u32[]{:S(2)}, u32[]{:S(2)}) collective-permute-start(bf16[256,128]{1,0:T(8,128)(2,1)S(1)} %get-tuple-element.67), channel_id=1, source_target_pairs={{127,0},{0,1},{1,2},{2,3},{3,4},{4,5},{5,6},{6,7},{7,8},{8,9},{9,1... | collective-permute-start | bytes 196616 | tf_op jit(solution)/shard_map/ppermute | solution.py:12
  80.7 17.1 %collective-permute-start.17 = (bf16[256,128]{1,0:T(8,128)(2,1)S(1)}, bf16[256,128]{1,0:T(8,128)(2,1)S(1)}, u32[]{:S(2)}, u32[]{:S(2)}) collective-permute-start(bf16[256,128]{1,0:T(8,128)(2,1)S(1)} %get-tuple-element.64), channel_id=1, source_target_pairs={{1,0},{2,1},{3,2},{4,3},{5,4},{6,5},{7,6},{8,7},{9,8},{10,9},{11,1... | collective-permute-start | bytes 196616 | tf_op jit(solution)/shard_map/ppermute | solution.py:12
  85.4 31.1 %collective-permute-start.5 = (bf16[256,128]{1,0:T(8,128)(2,1)S(1)}, bf16[256,128]{1,0:T(8,128)(2,1)S(1)}, u32[]{:S(2)}, u32[]{:S(2)}) collective-permute-start(bf16[256,128]{1,0:T(8,128)(2,1)S(1)} %get-tuple-element.65), channel_id=1, source_target_pairs={{1,0},{2,1},{3,2},{4,3},{5,4},{6,5},{7,6},{8,7},{9,8},{10,9},{11,1... | collective-permute-start | bytes 196616 | tf_op jit(solution)/shard_map/ppermute | solution.py:12
  97.7 18.8 %collective-permute-start.6 = (bf16[256,128]{1,0:T(8,128)(2,1)}, bf16[256,128]{1,0:T(8,128)(2,1)S(1)}, u32[]{:S(2)}, u32[]{:S(2)}) collective-permute-start(bf16[256,128]{1,0:T(8,128)(2,1)} %get-tuple-element.63), channel_id=1, source_target_pairs={{120,0},{121,1},{122,2},{123,3},{124,4},{125,5},{126,6},{127,7},{0... | collective-permute-start | bytes 196616 | tf_op jit(solution)/shard_map/ppermute | solution.py:12
  195.5 173.1 %collective-permute-start.15 = (bf16[256,128]{1,0:T(8,128)(2,1)}, bf16[256,128]{1,0:T(8,128)(2,1)S(1)}, u32[]{:S(2)}, u32[]{:S(2)}) collective-permute-start(bf16[256,128]{1,0:T(8,128)(2,1)} %get-tuple-element.28), channel_id=1, source_target_pairs={{120,0},{121,1},{122,2},{123,3},{124,4},{125,5},{126,6},{127,7},{0... | collective-permute-start | bytes 196616 | tf_op jit(solution)/shard_map/ppermute | solution.py:12
  259.2 28.2 %collective-permute-start.22 = (bf16[256,128]{1,0:T(8,128)(2,1)S(1)}, bf16[256,128]{1,0:T(8,128)(2,1)}, u32[]{:S(2)}, u32[]{:S(2)}) collective-permute-start(bf16[256,128]{1,0:T(8,128)(2,1)S(1)} %bitcast.234), channel_id=1, source_target_pairs={{8,0},{9,1},{10,2},{11,3},{12,4},{13,5},{14,6},{15,7},{16,8},{17,9... | collective-permute-start | bytes 196616 | tf_op jit(solution)/shard_map/ppermute | solution.py:12
  264.1 32.0 %collective-permute-start.23 = (bf16[256,128]{1,0:T(8,128)(2,1)S(1)}, bf16[256,128]{1,0:T(8,128)(2,1)}, u32[]{:S(2)}, u32[]{:S(2)}) collective-permute-start(bf16[256,128]{1,0:T(8,128)(2,1)S(1)} %bitcast.233), channel_id=1, source_target_pairs={{120,0},{121,1},{122,2},{123,3},{124,4},{125,5},{126,6},{127,7},{0... | collective-permute-start | bytes 196616 | tf_op jit(solution)/shard_map/ppermute | solution.py:12
  264.1 18.7 %collective-permute-start.21 = (bf16[256,128]{1,0:T(8,128)(2,1)}, bf16[256,128]{1,0:T(8,128)(2,1)}, u32[]{:S(2)}, u32[]{:S(2)}) collective-permute-start(bf16[256,128]{1,0:T(8,128)(2,1)} %bitcast.56), channel_id=1, source_target_pairs={{127,0},{0,1},{1,2},{2,3},{3,4},{4,5},{5,6},{6,7},{7,8},{8,9},{9,1... | collective-permute-start | bytes 196616 | tf_op jit(solution)/shard_map/ppermute | solution.py:12
  273.3 66.7 %collective-permute-start.14 = (bf16[256,128]{1,0:T(8,128)(2,1)}, bf16[256,128]{1,0:T(8,128)(2,1)}, u32[]{:S(2)}, u32[]{:S(2)}) collective-permute-start(bf16[256,128]{1,0:T(8,128)(2,1)} %get-tuple-element.29), channel_id=1, source_target_pairs={{8,0},{9,1},{10,2},{11,3},{12,4},{13,5},{14,6},{15,7},{16,8},{17,9... | collective-permute-start | bytes 196616 | tf_op jit(solution)/shard_map/ppermute | solution.py:12
  282.8 62.0 %collective-permute-start.13 = (bf16[256,128]{1,0:T(8,128)(2,1)}, bf16[256,128]{1,0:T(8,128)(2,1)}, u32[]{:S(2)}, u32[]{:S(2)}) collective-permute-start(bf16[256,128]{1,0:T(8,128)(2,1)} %get-tuple-element.30), channel_id=1, source_target_pairs={{127,0},{0,1},{1,2},{2,3},{3,4},{4,5},{5,6},{6,7},{7,8},{8,9},{9,1... | collective-permute-start | bytes 196616 | tf_op jit(solution)/shard_map/ppermute | solution.py:12
  287.4 57.4 %collective-permute-start.12 = (bf16[256,128]{1,0:T(8,128)(2,1)}, bf16[256,128]{1,0:T(8,128)(2,1)}, u32[]{:S(2)}, u32[]{:S(2)}) collective-permute-start(bf16[256,128]{1,0:T(8,128)(2,1)} %get-tuple-element.31), channel_id=1, source_target_pairs={{1,0},{2,1},{3,2},{4,3},{5,4},{6,5},{7,6},{8,7},{9,8},{10,9},{11,1... | collective-permute-start | bytes 196616 | tf_op jit(solution)/shard_map/ppermute | solution.py:12
  339.9 45.1 %collective-permute-start.27 = (bf16[256,128]{1,0:T(8,128)(2,1)S(1)}, bf16[256,128]{1,0:T(8,128)(2,1)S(1)}, u32[]{:S(2)}, u32[]{:S(2)}) collective-permute-start(bf16[256,128]{1,0:T(8,128)(2,1)S(1)} %get-tuple-element.24), channel_id=1, source_target_pairs={{120,0},{121,1},{122,2},{123,3},{124,4},{125,5},{126,6},{127,7},{0... | collective-permute-start | bytes 196616 | tf_op jit(solution)/shard_map/ppermute | solution.py:12
  340.0 42.1 %collective-permute-start.26 = (bf16[256,128]{1,0:T(8,128)(2,1)S(1)}, bf16[256,128]{1,0:T(8,128)(2,1)S(1)}, u32[]{:S(2)}, u32[]{:S(2)}) collective-permute-start(bf16[256,128]{1,0:T(8,128)(2,1)S(1)} %get-tuple-element.25), channel_id=1, source_target_pairs={{8,0},{9,1},{10,2},{11,3},{12,4},{13,5},{14,6},{15,7},{16,8},{17,9... | collective-permute-start | bytes 196616 | tf_op jit(solution)/shard_map/ppermute | solution.py:12
  344.8 34.5 %collective-permute-start.25 = (bf16[256,128]{1,0:T(8,128)(2,1)S(1)}, bf16[256,128]{1,0:T(8,128)(2,1)S(1)}, u32[]{:S(2)}, u32[]{:S(2)}) collective-permute-start(bf16[256,128]{1,0:T(8,128)(2,1)S(1)} %get-tuple-element.26), channel_id=1, source_target_pairs={{127,0},{0,1},{1,2},{2,3},{3,4},{4,5},{5,6},{6,7},{7,8},{8,9},{9,1... | collective-permute-start | bytes 196616 | tf_op jit(solution)/shard_map/ppermute | solution.py:12
  344.8 31.4 %collective-permute-start.24 = (bf16[256,128]{1,0:T(8,128)(2,1)S(1)}, bf16[256,128]{1,0:T(8,128)(2,1)S(1)}, u32[]{:S(2)}, u32[]{:S(2)}) collective-permute-start(bf16[256,128]{1,0:T(8,128)(2,1)S(1)} %get-tuple-element.27), channel_id=1, source_target_pairs={{1,0},{2,1},{3,2},{4,3},{5,4},{6,5},{7,6},{8,7},{9,8},{10,9},{11,1... | collective-permute-start | bytes 196616 | tf_op jit(solution)/shard_map/ppermute | solution.py:12
  483.5 21.0 %collective-permute-start.30 = (bf16[256,128]{1,0:T(8,128)(2,1)S(1)}, bf16[256,128]{1,0:T(8,128)(2,1)S(1)}, u32[]{:S(2)}, u32[]{:S(2)}) collective-permute-start(bf16[256,128]{1,0:T(8,128)(2,1)S(1)} %bitcast.235), channel_id=1, source_target_pairs={{8,0},{9,1},{10,2},{11,3},{12,4},{13,5},{14,6},{15,7},{16,8},{17,9... | collective-permute-start | bytes 196616 | tf_op jit(solution)/shard_map/ppermute | solution.py:12
  483.5 25.9 %collective-permute-start.31 = (bf16[256,128]{1,0:T(8,128)(2,1)}, bf16[256,128]{1,0:T(8,128)(2,1)S(1)}, u32[]{:S(2)}, u32[]{:S(2)}) collective-permute-start(bf16[256,128]{1,0:T(8,128)(2,1)} %bitcast.81), channel_id=1, source_target_pairs={{120,0},{121,1},{122,2},{123,3},{124,4},{125,5},{126,6},{127,7},{0... | collective-permute-start | bytes 196616 | tf_op jit(solution)/shard_map/ppermute | solution.py:12
  485.0 14.7 %collective-permute-start.29 = (bf16[256,128]{1,0:T(8,128)(2,1)S(1)}, bf16[256,128]{1,0:T(8,128)(2,1)S(1)}, u32[]{:S(2)}, u32[]{:S(2)}) collective-permute-start(bf16[256,128]{1,0:T(8,128)(2,1)S(1)} %bitcast.236), channel_id=1, source_target_pairs={{127,0},{0,1},{1,2},{2,3},{3,4},{4,5},{5,6},{6,7},{7,8},{8,9},{9,1... | collective-permute-start | bytes 196616 | tf_op jit(solution)/shard_map/ppermute | solution.py:12
  (47 other events, 432.0 us)
Sparse Core Ops, SparseCore 0:
  517.3 148.3 all-reduce.1
where the time goes:
time: 682 us; the launch traced here: 675 us
  other arithmetic  241 us (35%)
  waiting for transfers between devices  147 us (22%)
  local copies, waits for them, and re-layouts  119 us (17%)
  starting transfers between devices  79.8 us (12%)
  matrix products  72 us (11%)
  between operations  15.9 us (2%)
    psum x1, waiting for transfers between devices, per_device(): lax.psum(jnp.stack([grad_zero, grad_one, grad_two, grad_three]), 'dom')  146 us
    scatter-add x2, other arithmetic, spread(): summed_rows = jnp.zeros((block_count, tile_size, feature_width), jnp.floa...  81.7 us
    ppermute x32, starting transfers between devices, from_behind(): return lax.ppermute(block, axis, route)  79.8 us
    scatter-add x4, other arithmetic, unpool_parts(): extended.at[member_rows[0]].add(masked).at[member_rows[1]].add(masked)  64.2 us
    reshape x2, local copies, waits for them, and re-layouts, spread(): partial_value.reshape(-1, tile_size, feature_width)  40.3 us
    scatter-add x8, other arithmetic, retract(): own_rows = own_rows.at[send_rows[index]].add(returned[index])  37.4 us
    dot_general x2, matrix products, spread(): jnp.einsum('bktu,bth->bkuh', tile_values, gradient.reshape(tile_values.sh...  27.4 us
    dot_general x2, matrix products, aggregate(): jnp.einsum('bktu,bkuh->bth', tile_values, blocks, preferred_element_type=...  21.9 us
  transfers between devices with their start and end apart: 33, of which 3 were waited for; matrix products, arithmetic and copies ran while one was open for 32% of the time, Pallas kernels for 0%

commit v1 on v0

v1 whole, which is shorter than its diff:
```python
import functools

import jax
import jax.numpy as jnp
from jax import lax
from jax.experimental import pallas as pl
from jax.experimental.pallas import tpu as pltpu
from jax.sharding import PartitionSpec as P

MESH = pl.DeviceIdType.MESH
OFFSETS = (1, -1, 8, -8)
F32, BF16, I32 = jnp.float32, jnp.bfloat16, jnp.int32
VMEM = pl.BlockSpec(memory_space=pltpu.VMEM)
SMEM = pl.BlockSpec(memory_space=pltpu.SMEM)
ANY = pl.BlockSpec(memory_space=pl.ANY)
DMA = pltpu.SemaphoreType.DMA
H = 128
T = 128
KT = 12
FB = 32
CB = 20
NF = FB * T
NC = CB * T
SEND = 256
HALO = 4 * SEND
QUAD = 4 * T
UNROLL = 16
NN = (((1,), (0,)), ((), ()))
NT = (((1,), (1,)), ((), ()))
TN = (((0,), (0,)), ((), ()))


def dot(a, b, how=NN):
    return lax.dot_general(a, b, how, preferred_element_type=F32)


def shape(dims, dtype):
    return jax.ShapeDtypeStruct(dims, dtype)


def params(mib=56, **more):
    return pltpu.CompilerParams(vmem_limit_bytes=mib * 2**20, **more)


def neighbour(me, n, offset):
    return lax.rem(me + (offset + n), n)


def greet(me, n):
    barrier = pltpu.get_barrier_semaphore()
    for offset in OFFSETS:
        pl.semaphore_signal(
            barrier, inc=1, device_id=(neighbour(me, n, offset),), device_id_type=MESH
        )
    return barrier


def remote(src, dst, send_sem, recv_sem, target):
    return pltpu.make_async_remote_copy(
        src_ref=src,
        dst_ref=dst,
        send_sem=send_sem,
        recv_sem=recv_sem,
        device_id=(target,),
        device_id_type=MESH,
    )


def index_copies(pairs, sem):
    copies = []
    for src, dst in pairs:
        width = src.shape[2]
        for j in range(src.shape[1]):
            copies.append((src.at[0, j], dst.at[pl.ds(j * width, width)]))
    return [pltpu.make_async_copy(a, b, sem.at[i]) for i, (a, b) in enumerate(copies)]


def loop(count, body, unroll=1):
    def step(i, carry):
        body(i)
        return carry

    lax.fori_loop(0, count, step, 0, unroll=unroll)


def gather_rows(index, first, source, target, count, width=1):
    def body(i):
        base = pl.multiple_of(i * UNROLL, UNROLL)
        rows = [
            source[pl.ds(index[first + base + u] * width, width), :]
            for u in range(UNROLL)
        ]
        for u in range(UNROLL):
            target[pl.ds((base + u) * width, width), :] = rows[u]

    loop(count // UNROLL, body)


def block_row(tiles, columns, blocks, b, first):
    lhs = jnp.concatenate([tiles[b, k] for k in range(KT)], axis=1)
    rhs = jnp.concatenate([blocks[columns[first + k]] for k in range(KT)], axis=0)
    return dot(lhs, rhs)


def spread_row(tiles, columns, grads_t, b, first, total):
    for k in range(KT):
        c = columns[first + k]
        total[c] = total[c] + dot(grads_t, tiles[b, k])


def tile_copies(source, buffer, sem, count):
    size = source.shape[0] // count
    return [
        pltpu.make_async_copy(
            source.at[pl.ds(i * size, size)], buffer.at[pl.ds(i * size, size)], sem.at[i]
        )
        for i in range(count)
    ]


def wait_tiles(source, buffer, sem, i, size):
    pltpu.make_async_copy(
        source.at[pl.ds(i * size, size)], buffer.at[pl.ds(i * size, size)], sem.at[i]
    ).wait()


def forward_kernel(
    n,
    values,
    cot,
    weights,
    columns,
    count,
    fine_halo,
    coarse_halo,
    pair_send,
    members,
    tiles,
    h1_out,
    gate_out,
    slope_out,
    own_out,
    halo_out,
    z0_out,
    dz1_out,
    buf,
    ext,
    rows32,
    pairs,
    cells,
    stage,
    send_fine,
    send_pair,
    recv_pair,
    send_coarse,
    recv_coarse,
    s_fine,
    s_coarse,
    s_pair,
    s_members,
    tile_sem,
    index_sem,
    send_sem,
    recv_sem,
):
    me = lax.axis_index("dom")
    barrier = greet(me, n)
    index = index_copies(
        [(fine_halo, s_fine), (coarse_halo, s_coarse), (pair_send, s_pair), (members, s_members)],
        index_sem,
    )
    for copy in index:
        copy.start()
    for copy in tile_copies(tiles, buf, tile_sem, 8):
        copy.start()

    def project(i):
        at = pl.ds(i * QUAD, QUAD)
        low = dot(values[at, :], weights[0]).astype(BF16)
        rows32[at, :] = low.astype(F32)
        ext[pl.ds(i * 4, 4)] = low.reshape(4, T, H)

    loop(NF // QUAD, project)
    for copy in index:
        copy.wait()
    pl.semaphore_wait(barrier, 4)

    targets = [neighbour(me, n, offset) for offset in OFFSETS]
    fine = []
    for j in range(4):
        gather_rows(s_fine, j * SEND, rows32, stage, SEND)
        send_fine[pl.ds(2 * j, 2)] = stage[:SEND, :].astype(BF16).reshape(2, T, H)
        copy = remote(
            send_fine.at[pl.ds(2 * j, 2)],
            ext.at[pl.ds(FB + 2 * j, 2)],
            send_sem.at[j],
            recv_sem.at[j],
            targets[j],
        )
        copy.start()
        fine.append(copy)

    def place_cot(i):
        pairs[pl.ds(i * 2 * QUAD + 1, QUAD, stride=2), :] = cot[pl.ds(i * QUAD, QUAD), :].astype(F32)

    loop(NF // QUAD, place_cot)
    for copy in fine:
        copy.wait()

    def level(i):
        wait_tiles(tiles, buf, tile_sem, i, 4)
        parts = []
        for q in range(4):
            b = i * 4 + q
            parts.append(block_row(buf, columns, ext, b, b * KT))
        summed = jnp.concatenate(parts, axis=0)
        sigma = jax.nn.sigmoid(summed)
        gate = (summed * sigma).astype(BF16)
        at = pl.ds(i * QUAD, QUAD)
        gate_out[at, :] = gate
        slope_out[at, :] = (sigma * (1.0 + summed * (1.0 - sigma))).astype(BF16)
        out = (values[at, :].astype(F32) + dot(gate, weights[1])).astype(BF16)
        h1_out[at, :] = out
        pairs[pl.ds(i * 2 * QUAD, QUAD, stride=2), :] = out.astype(F32)

    loop(8, level)

    paired = []
    for j in range(4):
        gather_rows(s_pair, j * SEND, pairs, stage, SEND, 2)
        send_pair[j] = stage[...].astype(BF16)
        copy = remote(
            send_pair.at[j], recv_pair.at[j], send_sem.at[4 + j], recv_sem.at[4 + j], targets[j]
        )
        copy.start()
        paired.append(copy)
    for j in range(4):
        paired[j].wait()
        pairs[pl.ds(2 * NF + j * 2 * SEND, 2 * SEND), :] = recv_pair[j].astype(F32)

    def pool(i):
        base = pl.multiple_of(i * UNROLL, UNROLL)
        first = [pairs[pl.ds(s_members[base + u] * 2, 2), :] for u in range(UNROLL)]
        second = [pairs[pl.ds(s_members[NC + base + u] * 2, 2), :] for u in range(UNROLL)]
        for u in range(UNROLL):
            cells[pl.ds((base + u) * 2, 2), :] = first[u] + second[u]

    loop(NC // UNROLL, pool)
    live = count[0]

    def pooled(i):
        at = pl.ds(i * QUAD, QUAD)
        row = lax.broadcasted_iota(I32, (QUAD, H), 0) + i * QUAD
        alive = row < live
        z0 = jnp.where(alive, cells[pl.ds(i * 2 * QUAD, QUAD, stride=2), :], 0.0).astype(BF16)
        z0_out[at, :] = z0
        dz1_out[at, :] = jnp.where(
            alive, cells[pl.ds(i * 2 * QUAD + 1, QUAD, stride=2), :], 0.0
        ).astype(BF16)
        low = dot(z0, weights[2]).astype(BF16)
        rows32[at, :] = low.astype(F32)
        own_out[pl.ds(i * 4, 4)] = low.reshape(4, T, H)

    loop(NC // QUAD, pooled)
    coarse = []
    for j in range(4):
        gather_rows(s_coarse, j * SEND, rows32, stage, SEND)
        send_coarse[pl.ds(2 * j, 2)] = stage[:SEND, :].astype(BF16).reshape(2, T, H)
        copy = remote(
            send_coarse.at[pl.ds(2 * j, 2)],
            recv_coarse.at[pl.ds(2 * j, 2)],
            send_sem.at[8 + j],
            recv_sem.at[8 + j],
            targets[j],
        )
        copy.start()
        coarse.append(copy)
    for copy in coarse:
        copy.wait()
    halo_out[...] = recv_coarse[...]


def forward(n, values, cot, weights, columns, count, fine_halo, coarse_halo, pair_send, members, tiles):
    return pl.pallas_call(
        functools.partial(forward_kernel, n),
        name="forward",
        out_shape=[
            shape((NF, H), BF16),
            shape((NF, H), BF16),
            shape((NF, H), BF16),
            shape((CB, T, H), BF16),
            shape((8, T, H), BF16),
            shape((NC, H), BF16),
            shape((NC, H), BF16),
        ],
        in_specs=[VMEM, VMEM, VMEM, SMEM, SMEM, ANY, ANY, ANY, ANY, ANY],
        out_specs=[VMEM] * 7,
        scratch_shapes=[
            pltpu.VMEM((FB, KT, T, T), BF16),
            pltpu.VMEM((FB + 8, T, H), BF16),
            pltpu.VMEM((NF, H), F32),
            pltpu.VMEM((2 * (NF + HALO), H), F32),
            pltpu.VMEM((2 * NC, H), F32),
            pltpu.VMEM((2 * SEND, H), F32),
            pltpu.VMEM((8, T, H), BF16),
            pltpu.VMEM((4, 2 * SEND, H), BF16),
            pltpu.VMEM((4, 2 * SEND, H), BF16),
            pltpu.VMEM((8, T, H), BF16),
            pltpu.VMEM((8, T, H), BF16),
            pltpu.SMEM((HALO,), I32),
            pltpu.SMEM((HALO,), I32),
            pltpu.SMEM((HALO,), I32),
            pltpu.SMEM((2 * NC,), I32),
            DMA((8,)),
            DMA((14,)),
            DMA((12,)),
            DMA((12,)),
        ],
        compiler_params=params(collective_id=0, has_side_effects=True),
    )(values, cot, weights, columns, count, fine_halo, coarse_halo, pair_send, members, tiles)


def rows_out(total, blocks, own_ref, halo_ref):
    def own(c):
        own_ref[pl.ds(c * T, T), :] = jnp.transpose(total[c])

    loop(blocks, own, 4)

    def halo(c):
        halo_ref[pl.ds(c * T, T), :] = jnp.transpose(total[blocks + c]).astype(BF16)

    loop(8, halo, 4)


def coarse_kernel(
    own,
    halo,
    z0,
    dz1,
    weights,
    columns,
    tiles,
    z1_out,
    dm_out,
    piece_out,
    update_out,
    buf,
    ext,
    gates,
    total,
    tile_sem,
):
    for copy in tile_copies(tiles, buf, tile_sem, 5):
        copy.start()
    ext[pl.ds(0, CB)] = own[...]
    ext[pl.ds(CB, 8)] = halo[...]
    total[...] = jnp.zeros_like(total)

    def level(i):
        wait_tiles(tiles, buf, tile_sem, i, 4)
        parts = []
        for q in range(4):
            b = i * 4 + q
            parts.append(block_row(buf, columns, ext, b, b * KT))
        summed = jnp.concatenate(parts, axis=0)
        sigma = jax.nn.sigmoid(summed)
        gate = (summed * sigma).astype(BF16)
        at = pl.ds(i * QUAD, QUAD)
        gates[at, :] = gate
        z1_out[at, :] = (z0[at, :].astype(F32) + dot(gate, weights[3])).astype(BF16)
        slope = sigma * (1.0 + summed * (1.0 - sigma))
        grads = (dot(dz1[at, :], weights[3], NT) * slope).astype(BF16)
        for q in range(4):
            b = i * 4 + q
            grads_t = jnp.transpose(grads[q * T : (q + 1) * T, :])
            spread_row(buf, columns, grads_t, b, b * KT, total)

    loop(CB // 4, level)
    rows_out(total, CB, dm_out, piece_out)
    update_out[...] = dot(gates[...], dz1[...], TN)


def coarse_level(own, halo, z0, dz1, weights, columns, tiles):
    return pl.pallas_call(
        coarse_kernel,
        name="coarse_level",
        out_shape=[
            shape((NC, H), BF16),
            shape((NC, H), F32),
            shape((HALO, H), BF16),
            shape((H, H), F32),
        ],
        in_specs=[VMEM, VMEM, VMEM, VMEM, VMEM, SMEM, ANY],
        out_specs=[VMEM] * 4,
        scratch_shapes=[
            pltpu.VMEM((CB, KT, T, T), BF16),
            pltpu.VMEM((CB + 8, T, H), BF16),
            pltpu.VMEM((NC, H), BF16),
            pltpu.VMEM((CB + 8, T, H), F32),
            DMA((5,)),
        ],
        compiler_params=params(),
    )(own, halo, z0, dz1, weights, columns, tiles)


def swap_kernel(n, pieces, arrived, send_sem, recv_sem):
    me = lax.axis_index("dom")
    barrier = greet(me, n)
    pl.semaphore_wait(barrier, 4)
    size = pieces.shape[0] // 4
    copies = [
        remote(
            pieces.at[pl.ds(j * size, size)],
            arrived.at[pl.ds(j * size, size)],
            send_sem.at[j],
            recv_sem.at[j],
            neighbour(me, n, -OFFSETS[j]),
        )
        for j in range(4)
    ]
    for copy in copies:
        copy.start()
    for copy in copies:
        copy.wait()


def send_back(n, pieces, number):
    return pl.pallas_call(
        functools.partial(swap_kernel, n),
        name="send_back" + str(number),
        out_shape=shape(pieces.shape, pieces.dtype),
        in_specs=[ANY],
        out_specs=ANY,
        scratch_shapes=[DMA((4,)), DMA((4,))],
        compiler_params=params(1, collective_id=number, has_side_effects=True),
    )(pieces)


def add_rows(index, arrived, rows):
    def body(i):
        base = pl.multiple_of(i * UNROLL, UNROLL)
        for u in range(UNROLL):
            at = pl.ds(index[base + u], 1)
            rows[at, :] = rows[at, :] + arrived[pl.ds(base + u, 1), :]

    loop(HALO // UNROLL, body)


def coarse_back_kernel(
    dm,
    arrived,
    z0,
    dz1,
    z1,
    weights,
    count,
    coarse_halo,
    members,
    message_out,
    lifted_out,
    away_out,
    rows,
    add,
    cells,
    lifted,
    s_coarse,
    s_members,
    index_sem,
):
    index = index_copies([(coarse_halo, s_coarse), (members, s_members)], index_sem)
    for copy in index:
        copy.start()
    rows[...] = dm[...]
    add[...] = arrived[...].astype(F32)
    lifted[...] = jnp.zeros_like(lifted)
    for copy in index:
        copy.wait()
    add_rows(s_coarse, add, rows)
    low = rows[...].astype(BF16)
    message_out[...] = dot(z0[...], low, TN)

    def grads(i):
        at = pl.ds(i * QUAD, QUAD)
        cells[pl.ds(i * 2 * QUAD, QUAD, stride=2), :] = z1[at, :].astype(F32)
        cells[pl.ds(i * 2 * QUAD + 1, QUAD, stride=2), :] = dz1[at, :].astype(F32) + dot(
            rows[at, :].astype(BF16), weights[2], NT
        )

    loop(NC // QUAD, grads)
    live = count[0]

    def place(base, size):
        values = [cells[pl.ds((base + u) * 2, 2), :] for u in range(size)]
        for u in range(size):
            lifted[pl.ds(pl.multiple_of(s_members[base + u] * 2, 2), 2), :] = values[u]
            lifted[pl.ds(pl.multiple_of(s_members[NC + base + u] * 2, 2), 2), :] = values[u]

    groups = live // UNROLL
    loop(groups, lambda i: place(pl.multiple_of(i * UNROLL, UNROLL), UNROLL))
    loop(live - groups * UNROLL, lambda i: place(groups * UNROLL + i, 1))
    lifted_out[...] = lifted[: 2 * NF, :].astype(BF16)
    away_out[...] = lifted[2 * NF :, :].astype(BF16)


def coarse_back(dm, arrived, z0, dz1, z1, weights, count, coarse_halo, members):
    return pl.pallas_call(
        coarse_back_kernel,
        name="coarse_back",
        out_shape=[shape((H, H), F32), shape((2 * NF, H), BF16), shape((2 * HALO, H), BF16)],
        in_specs=[VMEM] * 6 + [SMEM, ANY, ANY],
        out_specs=[VMEM] * 3,
        scratch_shapes=[
            pltpu.VMEM((NC, H), F32),
            pltpu.VMEM((HALO, H), F32),
            pltpu.VMEM((2 * NC, H), F32),
            pltpu.VMEM((2 * (NF + HALO), H), F32),
            pltpu.SMEM((HALO,), I32),
            pltpu.SMEM((2 * NC,), I32),
            DMA((6,)),
        ],
        compiler_params=params(),
    )(dm, arrived, z0, dz1, z1, weights, count, coarse_halo, members)


def fine_kernel(
    lifted,
    returned,
    h1,
    cot,
    gate,
    slope,
    weights,
    columns,
    pair_send,
    tiles,
    result_out,
    low_out,
    dm_out,
    piece_out,
    update_out,
    buf,
    pairs,
    add,
    total,
    s_pair,
    index_sem,
    tile_sem,
):
    index = index_copies([(pair_send, s_pair)], index_sem)
    for copy in index:
        copy.start()
    for copy in tile_copies(tiles, buf, tile_sem, 8):
        copy.start()
    pairs[...] = lifted[...].astype(F32)
    add[...] = returned[...].astype(F32)
    total[...] = jnp.zeros_like(total)
    update_out[...] = jnp.zeros_like(update_out)
    for copy in index:
        copy.wait()

    def place(i):
        base = pl.multiple_of(i * UNROLL, UNROLL)
        at = [pl.ds(pl.multiple_of(s_pair[base + u] * 2, 2), 2) for u in range(UNROLL)]
        values = [pairs[at[u], :] + add[pl.ds((base + u) * 2, 2), :] for u in range(UNROLL)]
        for u in range(UNROLL):
            pairs[at[u], :] = values[u]

    loop(HALO // UNROLL, place)

    def level(i):
        at = pl.ds(i * QUAD, QUAD)
        result_out[at, :] = (
            h1[at, :].astype(F32) + pairs[pl.ds(i * 2 * QUAD, QUAD, stride=2), :]
        ).astype(BF16)
        low = (
            cot[at, :].astype(F32) + pairs[pl.ds(i * 2 * QUAD + 1, QUAD, stride=2), :]
        ).astype(BF16)
        low_out[at, :] = low
        update_out[...] += dot(gate[at, :], low, TN)
        grads = (dot(low, weights[1], NT) * slope[at, :].astype(F32)).astype(BF16)
        wait_tiles(tiles, buf, tile_sem, i, 4)
        for q in range(4):
            b = i * 4 + q
            grads_t = jnp.transpose(grads[q * T : (q + 1) * T, :])
            spread_row(buf, columns, grads_t, b, b * KT, total)

    loop(8, level)
    rows_out(total, FB, dm_out, piece_out)


def fine_level(lifted, returned, h1, cot, gate, slope, weights, columns, pair_send, tiles):
    return pl.pallas_call(
        fine_kernel,
        name="fine_level",
        out_shape=[
            shape((NF, H), BF16),
            shape((NF, H), BF16),
            shape((NF, H), F32),
            shape((HALO, H), BF16),
            shape((H, H), F32),
        ],
        in_specs=[VMEM] * 7 + [SMEM, ANY, ANY],
        out_specs=[VMEM] * 5,
        scratch_shapes=[
            pltpu.VMEM((FB, KT, T, T), BF16),
            pltpu.VMEM((2 * NF, H), F32),
            pltpu.VMEM((2 * HALO, H), F32),
            pltpu.VMEM((FB + 8, T, H), F32),
            pltpu.SMEM((HALO,), I32),
            DMA((4,)),
            DMA((8,)),
        ],
        compiler_params=params(),
    )(lifted, returned, h1, cot, gate, slope, weights, columns, pair_send, tiles)


def fine_back_kernel(
    dm, arrived, values, low, weights, fine_halo, grad_out, message_out, rows, add, s_fine, index_sem
):
    index = index_copies([(fine_halo, s_fine)], index_sem)
    for copy in index:
        copy.start()
    rows[...] = dm[...]
    add[...] = arrived[...].astype(F32)
    message_out[...] = jnp.zeros_like(message_out)
    for copy in index:
        copy.wait()
    add_rows(s_fine, add, rows)

    def grads(i):
        at = pl.ds(i * QUAD, QUAD)
        part = rows[at, :].astype(BF16)
        message_out[...] += dot(values[at, :], part, TN)
        grad_out[at, :] = (low[at, :].astype(F32) + dot(part, weights[0], NT)).astype(BF16)

    loop(8, grads)


def fine_back(dm, arrived, values, low, weights, fine_halo):
    return pl.pallas_call(
        fine_back_kernel,
        name="fine_back",
        out_shape=[shape((NF, H), BF16), shape((H, H), F32)],
        in_specs=[VMEM] * 5 + [ANY],
        out_specs=[VMEM] * 2,
        scratch_shapes=[
            pltpu.VMEM((NF, H), F32),
            pltpu.VMEM((HALO, H), F32),
            pltpu.SMEM((HALO,), I32),
            DMA((4,)),
        ],
        compiler_params=params(),
    )(dm, arrived, values, low, weights, fine_halo)


NEAR = 8
FAR = 16


def total_kernel(
    n,
    m0,
    u0,
    m1,
    u1,
    out_ref,
    grads,
    near,
    part,
    far,
    whole,
    sum_send,
    sum_recv,
    far_send,
    far_recv,
    all_send,
    all_recv,
):
    me = lax.axis_index("dom")
    group, rank = me // NEAR, me % NEAR
    close = [group * NEAR + (rank + s) % NEAR for s in range(1, NEAR)]
    distant = [((group + s) % FAR) * NEAR + rank for s in range(1, FAR)]
    barrier = pltpu.get_barrier_semaphore()
    for target in close + distant:
        pl.semaphore_signal(barrier, inc=1, device_id=(target,), device_id_type=MESH)
    for i, ref in enumerate((m0, u0, m1, u1)):
        grads[pl.ds(i * H, H), :] = ref[...]
    pl.semaphore_wait(barrier, NEAR - 1 + FAR - 1)
    size = 4 * H // NEAR
    copies = []
    for s in range(NEAR - 1):
        theirs = (rank + s + 1) % NEAR
        copies.append(
            remote(
                grads.at[pl.ds(theirs * size, size)],
                near.at[s],
                sum_send.at[s],
                sum_recv.at[s],
                close[s],
            )
        )
    for copy in copies:
        copy.start()
    for copy in copies:
        copy.wait()
    summed = grads[pl.ds(rank * size, size), :]
    for s in range(NEAR - 1):
        summed = summed + near[s]
    part[...] = summed
    far[group] = summed
    copies = [
        remote(part, far.at[group], far_send.at[s], far_recv.at[s], distant[s])
        for s in range(FAR - 1)
    ]
    for copy in copies:
        copy.start()
    for copy in copies:
        copy.wait()
    summed = far[0]
    for s in range(1, FAR):
        summed = summed + far[s]
    mine = pl.ds(rank * size, size)
    whole[mine, :] = summed
    copies = [
        remote(whole.at[mine], whole.at[mine], all_send.at[s], all_recv.at[s], close[s])
        for s in range(NEAR - 1)
    ]
    for copy in copies:
        copy.start()
    for copy in copies:
        copy.wait()
    out_ref[...] = whole[...].reshape(4, H, H)


def grand_total(n, m0, u0, m1, u1, number):
    size = 4 * H // NEAR
    return pl.pallas_call(
        functools.partial(total_kernel, n),
        name="grand_total",
        out_shape=shape((4, H, H), F32),
        in_specs=[VMEM] * 4,
        out_specs=VMEM,
        scratch_shapes=[
            pltpu.VMEM((4 * H, H), F32),
            pltpu.VMEM((NEAR - 1, size, H), F32),
            pltpu.VMEM((size, H), F32),
            pltpu.VMEM((FAR, size, H), F32),
            pltpu.VMEM((4 * H, H), F32),
            DMA((NEAR - 1,)),
            DMA((NEAR - 1,)),
            DMA((FAR - 1,)),
            DMA((FAR - 1,)),
            DMA((NEAR - 1,)),
            DMA((NEAR - 1,)),
        ],
        compiler_params=params(8, collective_id=number, has_side_effects=True),
    )(m0, u0, m1, u1)


def per_device(
    n,
    features,
    cotangent,
    weights,
    fine_tiles,
    fine_columns,
    fine_halo,
    coarse_tiles,
    coarse_columns,
    coarse_halo,
    pair_send,
    members,
    coarse_count,
):
    fine_cols = fine_columns.reshape(-1)
    coarse_cols = coarse_columns.reshape(-1)
    h1, gate, slope, own, halo, z0, dz1 = forward(
        n,
        features,
        cotangent,
        weights,
        fine_cols,
        coarse_count,
        fine_halo,
        coarse_halo,
        pair_send,
        members,
        fine_tiles,
    )
    z1, dm1, piece1, update1 = coarse_level(own, halo, z0, dz1, weights, coarse_cols, coarse_tiles)
    arrived1 = send_back(n, piece1, 1)
    message1, lifted, away = coarse_back(
        dm1, arrived1, z0, dz1, z1, weights, coarse_count, coarse_halo, members
    )
    returned = send_back(n, away, 2)
    result, low, dm0, piece0, update0 = fine_level(
        lifted, returned, h1, cotangent, gate, slope, weights, fine_cols, pair_send, fine_tiles
    )
    arrived0 = send_back(n, piece0, 3)
    grad_features, message0 = fine_back(dm0, arrived0, features, low, weights, fine_halo)
    grads = grand_total(n, message0, update0, message1, update1, 4)
    return result, grad_features, grads


def solution(mesh):
    n = mesh.shape["dom"]
    placed = (
        P("dom", None),
        P("dom", None),
        P(),
        P("dom", None, None, None),
        P("dom", None, None),
        P("dom", None, None),
        P("dom", None, None, None),
        P("dom", None, None),
        P("dom", None, None),
        P("dom", None, None),
        P("dom", None, None),
        P("dom"),
    )
    return jax.shard_map(
        functools.partial(per_device, n),
        mesh=mesh,
        in_specs=placed,
        out_specs=(P("dom", None), P("dom", None), P()),
        check_vma=False,
    )
```

time: 682 us -> 158 us (0.23); the launches traced: 675 us -> 158 us
  other arithmetic: 241 us -> 0 us
  Pallas kernels: 0 us -> 147 us
  waiting for transfers between devices: 147 us -> 0 us
  local copies, waits for them, and re-layouts: 119 us -> 9.57 us
  starting transfers between devices: 79.8 us -> 0 us
  matrix products: 72 us -> 0 us
  between operations: 15.9 us -> 1.43 us
    scatter-add x22 -> x0, other arithmetic: 215 us -> none  [the longest x2 81.7 us: spread(): summed_rows = jnp.zeros((block_count, tile_size, feature_width), jnp.floa...]
    pallas_call x0 -> x9, Pallas kernels: none -> 147 us  [the longest x1 42.1 us: forward(): pl.pallas_call(functools.partial(forward_kernel, n), name='forward', out_...]
    psum x1 -> x0, waiting for transfers between devices: 146 us -> none  [per_device(): lax.psum(jnp.stack([grad_zero, grad_one, grad_two, grad_three]), 'dom')]
    ppermute x32 -> x0, starting transfers between devices: 79.8 us -> none  [from_behind(): return lax.ppermute(block, axis, route)]
    dot_general x16 -> x0, matrix products: 72 us -> none  [the longest x2 27.4 us: spread(): jnp.einsum('bktu,bth->bkuh', tile_values, gradient.reshape(tile_values.sh...]
    gather x22 -> x0, local copies, waits for them, and re-layouts: 66.2 us -> none  [the longest x2 19.7 us: aggregate(): blocks = extended.reshape(-1, tile_size, feature_width)[columns]]
    reshape x2, local copies, waits for them, and re-layouts: 40.3 us -> 1.36 us  [the longest x1 0.7 us: per_device(): fine_cols = fine_columns.reshape(-1)]
    convert_element_type x4 -> x0, other arithmetic: 10.4 us -> none  [the longest x2 5.53 us: level_rest(): gated_rows = jax.nn.silu(summed).astype(jnp.bfloat16)]
  transfers between devices with their start and end apart: 33 -> 0, of which waited for: 3 -> 0; matrix products, arithmetic and copies ran while one was open for 32% -> 0% of each run, Pallas kernels for 0% -> 0%
where the time goes in v1:
time: 158 us
  Pallas kernels  147 us (93%)
  local copies, waits for them, and re-layouts  9.57 us (6%)
    pallas_call x1, Pallas kernels, forward(): pl.pallas_call(functools.partial(forward_kernel, n), name='forward', out_...  42.1 us
    pallas_call x3, Pallas kernels, send_back(): pl.pallas_call(functools.partial(swap_kernel, n), name='send_back' + str(...  29 us
    pallas_call x1, Pallas kernels, grand_total(): pl.pallas_call(functools.partial(total_kernel, n), name='grand_total', ou...  23.9 us
    pallas_call x1, Pallas kernels, fine_level(): pl.pallas_call(fine_kernel, name='fine_level', out_shape=[shape((NF, H),...  16.8 us
    pallas_call x1, Pallas kernels, coarse_back(): pl.pallas_call(coarse_back_kernel, name='coarse_back', out_shape=[shape((...  14.1 us
    pallas_call x1, Pallas kernels, coarse_level(): pl.pallas_call(coarse_kernel, name='coarse_level', out_shape=[shape((NC,...  11.3 us
    pallas_call x1, Pallas kernels, fine_back(): pl.pallas_call(fine_back_kernel, name='fine_back', out_shape=[shape((NF,...  9.63 us
    unnamed x23, local copies, waits for them, and re-layouts  8.21 us

profile of v1, /device:TPU:1, one launch (start us, length us, event | category | flops | bytes accessed | tf_op | source)
XLA Modules:
  0.0 157.8 jit_solution(9001657981167685993)
XLA Ops:
  1.3 0.8 copy.16
  2.1 0.7 reshape.13.columns
  2.7 0.8 copy.15
  3.5 0.7 reshape.12.columns
  4.2 42.1 %forward.1 = (bf16[4096,128]{1,0:T(8,128)(2,1)}, bf16[4096,128]{1,0:T(8,128)(2,1)}, bf16[4096,128]{1,0:T(8,128)(2,1)}, bf16[20,128,128]{2,1,0:T(8,128)(2,1)}, bf...) custom-call(bf16[4096,128]{1,0:T(8,128)(2,1)} %values.3, bf16[4096,128]{1,0:T(8,128)(2,1)} %cot.3, ...), custom_call_target="tpu_custom_call" | custom-call | tf_op jit(solution)/shard_map/forward/pallas_call | solution.py:284
  46.3 11.3 %coarse_level.1 = (bf16[2560,128]{1,0:T(8,128)(2,1)}, f32[2560,128]{1,0:T(8,128)}, bf16[1024,128]{1,0:T(8,128)(2,1)}, f32[128,128]{1,0:T(8,128)}) custom-call(bf16[20,128,128]{2,1,0:T(8,128)(2,1)} %get-tuple-element.24.own, bf16[8,128,128]{2,1,0:T(8,128)(2,1)} %get-tuple-element.25.halo, bf16[2560,128]{1,0:T(8,128)(2,1)} %get-tuple-element.26.z0, ...), custom_call_target="tpu_custom_call" | custom-call | tf_op jit(solution)/shard_map/coarse_level/pallas_call | solution.py:384
  57.6 0.0 copy-start.5
  57.6 0.9 copy-done.5
  58.5 9.5 %send_back1.1.arrived = bf16[1024,128]{1,0:T(8,128)(2,1)S(1)} custom-call(bf16[1024,128]{1,0:T(8,128)(2,1)S(1)} %copy-done.5), custom_call_target="tpu_custom_call" | custom-call | tf_op jit(solution)/shard_map/send_back1/pallas_call | solution.py:428
  68.0 0.0 copy-start.1
  68.0 0.7 copy-done.1
  68.7 14.1 %coarse_back.1 = (f32[128,128]{1,0:T(8,128)}, bf16[8192,128]{1,0:T(8,128)(2,1)}, bf16[2048,128]{1,0:T(8,128)(2,1)}) custom-call(f32[2560,128]{1,0:T(8,128)} %get-tuple-element.28.dm, bf16[1024,128]{1,0:T(8,128)(2,1)} %copy-done.1, bf16[2560,128]{1,0:T(8,128)(2,1)} %get-tuple-element.26.z0, bf16[2560,128]{1,0:T(8,128)(2,1)} %get-tuple-element.27.dz1, ...), custom_call_target="tpu_custom_call" | custom-call | tf_op jit(solution)/shard_map/coarse_back/pallas_call | solution.py:506
  82.9 1.0 copy-done.3
  83.9 10.1 %send_back2.1.returned = bf16[2048,128]{1,0:T(8,128)(2,1)S(1)} custom-call(bf16[2048,128]{1,0:T(8,128)(2,1)S(1)} %copy-done.3), custom_call_target="tpu_custom_call" | custom-call | tf_op jit(solution)/shard_map/send_back2/pallas_call | solution.py:428
  94.0 0.8 copy-done
  94.8 16.8 %fine_level.1 = (bf16[4096,128]{1,0:T(8,128)(2,1)}, bf16[4096,128]{1,0:T(8,128)(2,1)}, f32[4096,128]{1,0:T(8,128)}, bf16[1024,128]{1,0:T(8,128)(2,1)}, f32[128,128]{1,0:T(8,128)}) custom-call(bf16[8192,128]{1,0:T(8,128)(2,1)} %get-tuple-element.31.lifted, bf16[2048,128]{1,0:T(8,128)(2,1)} %copy-done, bf16[4096,128]{1,0:T(8,128)(2,1)} %get-tuple-element.33.h1, ...), custom_call_target="tpu_custom_call" | custom-call | tf_op jit(solution)/shard_map/fine_level/pallas_call | solution.py:592
  111.6 0.0 copy-start.4
  111.6 0.9 copy-done.4
  112.5 9.4 %send_back3.1.arrived = bf16[1024,128]{1,0:T(8,128)(2,1)S(1)} custom-call(bf16[1024,128]{1,0:T(8,128)(2,1)S(1)} %copy-done.4), custom_call_target="tpu_custom_call" | custom-call | tf_op jit(solution)/shard_map/send_back3/pallas_call | solution.py:428
  122.0 0.7 copy-done.2
  122.7 9.6 %fine_back.1 = (bf16[4096,128]{1,0:T(8,128)(2,1)}, f32[128,128]{1,0:T(8,128)}) custom-call(f32[4096,128]{1,0:T(8,128)} %get-tuple-element.37.dm, bf16[1024,128]{1,0:T(8,128)(2,1)} %copy-done.2, bf16[4096,128]{1,0:T(8,128)(2,1)} %values.3, bf16[4096,128]{1,0:T(8,128)(2,1)} %get-tuple-element.39.low, bf16[4,128,128]{2,1,0:T(8,128)(2,1)} %weights.9, ...), custom_call_target="tpu_custom_call" | custom-call | tf_op jit(solution)/shard_map/fine_back/pallas_call | solution.py:640
  132.4 0.8 copy-done.9
  133.2 23.9 %grand_total.1 = f32[4,128,128]{2,1,0:T(8,128)S(1)} custom-call(f32[128,128]{1,0:T(8,128)S(1)} %copy-done.9, f32[128,128]{1,0:T(8,128)S(1)} %copy-done.8, f32[128,128]{1,0:T(8,128)S(1)} %copy-done.7, f32[128,128]{1,0:T(8,128)S(1)} %copy-done.6), custom_call_target="tpu_custom_call" | custom-call | tf_op jit(solution)/shard_map/grand_total/pallas_call | solution.py:737
  157.1 0.7 copy.19
  (10 shorter events, 0.0 us)
Async XLA Ops:
  57.6 1.0 copy-start.5
  68.0 0.7 copy-start.1
  82.8 1.0 copy-start.3
  94.0 0.8 copy-start
  111.6 1.0 copy-start.4
  122.0 0.7 copy-start.2
  122.7 9.7 %copy-start.6 = (f32[128,128]{1,0:T(8,128)S(1)}, f32[128,128]{1,0:T(8,128)}, u32[]{:S(2)}) copy-start(f32[128,128]{1,0:T(8,128)} %get-tuple-element.44.u1) | copy-start | bytes 196612
  122.7 9.7 %copy-start.7 = (f32[128,128]{1,0:T(8,128)S(1)}, f32[128,128]{1,0:T(8,128)}, u32[]{:S(2)}) copy-start(f32[128,128]{1,0:T(8,128)} %get-tuple-element.43.m1) | copy-start | bytes 196612
  122.7 9.7 %copy-start.8 = (f32[128,128]{1,0:T(8,128)S(1)}, f32[128,128]{1,0:T(8,128)}, u32[]{:S(2)}) copy-start(f32[128,128]{1,0:T(8,128)} %get-tuple-element.42.u0) | copy-start | bytes 196612
  132.3 0.8 copy-start.9

commit v2 on v1

v2 whole, which is shorter than its diff:
```python
import functools

import jax
import jax.numpy as jnp
from jax import lax
from jax.experimental import pallas as pl
from jax.experimental.pallas import tpu as pltpu
from jax.sharding import PartitionSpec as P

MESH = pl.DeviceIdType.MESH
OFFSETS = (1, -1, 8, -8)
F32, BF16, I32 = jnp.float32, jnp.bfloat16, jnp.int32
VMEM = pl.BlockSpec(memory_space=pltpu.VMEM)
SMEM = pl.BlockSpec(memory_space=pltpu.SMEM)
ANY = pl.BlockSpec(memory_space=pl.ANY)
DMA = pltpu.SemaphoreType.DMA
H = 128
T = 128
KT = 12
FB = 32
CB = 20
NF = FB * T
NC = CB * T
SEND = 256
HALO = 4 * SEND
QUAD = 4 * T
UNROLL = 16
NN = (((1,), (0,)), ((), ()))
NT = (((1,), (1,)), ((), ()))
TN = (((0,), (0,)), ((), ()))


def dot(a, b, how=NN):
    return lax.dot_general(a, b, how, preferred_element_type=F32)


def shape(dims, dtype):
    return jax.ShapeDtypeStruct(dims, dtype)


def params(mib=56, **more):
    return pltpu.CompilerParams(vmem_limit_bytes=mib * 2**20, **more)


def neighbour(me, n, offset):
    return lax.rem(me + (offset + n), n)


def greet(me, n):
    barrier = pltpu.get_barrier_semaphore()
    for offset in OFFSETS:
        pl.semaphore_signal(
            barrier, inc=1, device_id=(neighbour(me, n, offset),), device_id_type=MESH
        )
    return barrier


def remote(src, dst, send_sem, recv_sem, target):
    return pltpu.make_async_remote_copy(
        src_ref=src,
        dst_ref=dst,
        send_sem=send_sem,
        recv_sem=recv_sem,
        device_id=(target,),
        device_id_type=MESH,
    )


def index_copies(pairs, sem):
    copies = []
    for src, dst in pairs:
        width = src.shape[2]
        for j in range(src.shape[1]):
            copies.append((src.at[0, j], dst.at[pl.ds(j * width, width)]))
    return [pltpu.make_async_copy(a, b, sem.at[i]) for i, (a, b) in enumerate(copies)]


def loop(count, body, unroll=1):
    def step(i, carry):
        body(i)
        return carry

    lax.fori_loop(0, count, step, 0, unroll=unroll)


def gather_rows(index, first, source, target, count, step=1, shift=0):
    def body(i):
        base = pl.multiple_of(i * UNROLL, UNROLL)
        rows = [
            source[pl.ds(index[first + base + u] * step + shift, 1), :] for u in range(UNROLL)
        ]
        for u in range(UNROLL):
            target[pl.ds(base + u, 1), :] = rows[u]

    loop(count // UNROLL, body)


def block_row(tiles, columns, blocks, b):
    lhs = jnp.concatenate([tiles[b, k] for k in range(KT)], axis=1)
    rhs = jnp.concatenate([blocks[columns[k, 0, b]] for k in range(KT)], axis=0)
    return dot(lhs, rhs)


def spread_row(tiles, columns, grads_t, b, total):
    for k in range(KT):
        c = columns[k, 0, b]
        total[c] = total[c] + dot(grads_t, tiles[b, k])


def tile_copies(source, buffer, sem, count):
    size = source.shape[0] // count
    return [
        pltpu.make_async_copy(
            source.at[pl.ds(i * size, size)], buffer.at[pl.ds(i * size, size)], sem.at[i]
        )
        for i in range(count)
    ]


def wait_tiles(source, buffer, sem, i, size):
    pltpu.make_async_copy(
        source.at[pl.ds(i * size, size)], buffer.at[pl.ds(i * size, size)], sem.at[i]
    ).wait()


def forward_kernel(
    n,
    values,
    cot,
    weights,
    columns_hbm,
    count,
    fine_halo,
    coarse_halo,
    pair_send,
    members,
    tiles,
    h1_out,
    gate_out,
    slope_out,
    own_out,
    halo_out,
    z0_out,
    dz1_out,
    buf,
    ext,
    rows32,
    pairs,
    cells,
    stage,
    send_fine,
    send_cot,
    recv_cot,
    send_pair,
    recv_pair,
    send_coarse,
    recv_coarse,
    s_fine,
    s_coarse,
    s_pair,
    s_members,
    columns,
    tile_sem,
    index_sem,
    send_sem,
    recv_sem,
):
    me = lax.axis_index("dom")
    barrier = greet(me, n)
    index = index_copies(
        [(fine_halo, s_fine), (coarse_halo, s_coarse), (pair_send, s_pair), (members, s_members)],
        index_sem,
    )
    index.append(pltpu.make_async_copy(columns_hbm, columns, index_sem.at[14]))
    for copy in index:
        copy.start()
    for copy in tile_copies(tiles, buf, tile_sem, 8):
        copy.start()

    def project(i):
        at = pl.ds(i * QUAD, QUAD)
        low = dot(values[at, :], weights[0]).astype(BF16)
        rows32[at, :] = low.astype(F32)
        ext[pl.ds(i * 4, 4)] = low.reshape(4, T, H)

    loop(NF // QUAD, project)
    for copy in index:
        copy.wait()
    pl.semaphore_wait(barrier, 4)

    targets = [neighbour(me, n, offset) for offset in OFFSETS]
    fine = []
    for j in range(4):
        gather_rows(s_fine, j * SEND, rows32, stage, SEND)
        send_fine[pl.ds(2 * j, 2)] = stage[:SEND, :].astype(BF16).reshape(2, T, H)
        copy = remote(
            send_fine.at[pl.ds(2 * j, 2)],
            ext.at[pl.ds(FB + 2 * j, 2)],
            send_sem.at[j],
            recv_sem.at[j],
            targets[j],
        )
        copy.start()
        fine.append(copy)

    def place_cot(i):
        pairs[pl.ds(i * 2 * QUAD + 1, QUAD, stride=2), :] = cot[pl.ds(i * QUAD, QUAD), :].astype(F32)

    loop(NF // QUAD, place_cot)

    def exchange_pairs(shift, sent, received, first):
        copies = []
        for j in range(4):
            gather_rows(s_pair, j * SEND, pairs, stage, SEND, 2, shift)
            sent[j] = stage[:SEND, :].astype(BF16)
            copy = remote(
                sent.at[j],
                received.at[j],
                send_sem.at[first + j],
                recv_sem.at[first + j],
                targets[j],
            )
            copy.start()
            copies.append(copy)
        return copies

    paired_cot = exchange_pairs(1, send_cot, recv_cot, 12)
    for copy in fine:
        copy.wait()

    def level(i):
        wait_tiles(tiles, buf, tile_sem, i, 4)
        parts = []
        for q in range(4):
            b = i * 4 + q
            parts.append(block_row(buf, columns, ext, b))
        summed = jnp.concatenate(parts, axis=0)
        sigma = jax.nn.sigmoid(summed)
        gate = (summed * sigma).astype(BF16)
        at = pl.ds(i * QUAD, QUAD)
        gate_out[at, :] = gate
        slope_out[at, :] = (sigma * (1.0 + summed * (1.0 - sigma))).astype(BF16)
        out = (values[at, :].astype(F32) + dot(gate, weights[1])).astype(BF16)
        h1_out[at, :] = out
        pairs[pl.ds(i * 2 * QUAD, QUAD, stride=2), :] = out.astype(F32)

    loop(8, level)

    paired = exchange_pairs(0, send_pair, recv_pair, 4)
    for shift, copies, received in ((1, paired_cot, recv_cot), (0, paired, recv_pair)):
        for j in range(4):
            copies[j].wait()
            pairs[pl.ds(2 * (NF + j * SEND) + shift, SEND, stride=2), :] = received[j].astype(F32)

    def pool(i):
        base = pl.multiple_of(i * UNROLL, UNROLL)
        first = [pairs[pl.ds(s_members[base + u] * 2, 2), :] for u in range(UNROLL)]
        second = [pairs[pl.ds(s_members[NC + base + u] * 2, 2), :] for u in range(UNROLL)]
        for u in range(UNROLL):
            cells[pl.ds((base + u) * 2, 2), :] = first[u] + second[u]

    loop(NC // UNROLL, pool)
    live = count[0]

    def pooled(i):
        at = pl.ds(i * QUAD, QUAD)
        row = lax.broadcasted_iota(I32, (QUAD, H), 0) + i * QUAD
        alive = row < live
        z0 = jnp.where(alive, cells[pl.ds(i * 2 * QUAD, QUAD, stride=2), :], 0.0).astype(BF16)
        z0_out[at, :] = z0
        dz1_out[at, :] = jnp.where(
            alive, cells[pl.ds(i * 2 * QUAD + 1, QUAD, stride=2), :], 0.0
        ).astype(BF16)
        low = dot(z0, weights[2]).astype(BF16)
        rows32[at, :] = low.astype(F32)
        own_out[pl.ds(i * 4, 4)] = low.reshape(4, T, H)

    loop(NC // QUAD, pooled)
    coarse = []
    for j in range(4):
        gather_rows(s_coarse, j * SEND, rows32, stage, SEND)
        send_coarse[pl.ds(2 * j, 2)] = stage[:SEND, :].astype(BF16).reshape(2, T, H)
        copy = remote(
            send_coarse.at[pl.ds(2 * j, 2)],
            recv_coarse.at[pl.ds(2 * j, 2)],
            send_sem.at[8 + j],
            recv_sem.at[8 + j],
            targets[j],
        )
        copy.start()
        coarse.append(copy)
    for copy in coarse:
        copy.wait()
    halo_out[...] = recv_coarse[...]


def forward(n, values, cot, weights, columns, count, fine_halo, coarse_halo, pair_send, members, tiles):
    return pl.pallas_call(
        functools.partial(forward_kernel, n),
        name="forward",
        out_shape=[
            shape((NF, H), BF16),
            shape((NF, H), BF16),
            shape((NF, H), BF16),
            shape((CB, T, H), BF16),
            shape((8, T, H), BF16),
            shape((NC, H), BF16),
            shape((NC, H), BF16),
        ],
        in_specs=[VMEM, VMEM, VMEM, ANY, SMEM, ANY, ANY, ANY, ANY, ANY],
        out_specs=[VMEM] * 7,
        scratch_shapes=[
            pltpu.VMEM((FB, KT, T, T), BF16),
            pltpu.VMEM((FB + 8, T, H), BF16),
            pltpu.VMEM((NF, H), F32),
            pltpu.VMEM((2 * (NF + HALO), H), F32),
            pltpu.VMEM((2 * NC, H), F32),
            pltpu.VMEM((2 * SEND, H), F32),
            pltpu.VMEM((8, T, H), BF16),
            pltpu.VMEM((4, SEND, H), BF16),
            pltpu.VMEM((4, SEND, H), BF16),
            pltpu.VMEM((4, SEND, H), BF16),
            pltpu.VMEM((4, SEND, H), BF16),
            pltpu.VMEM((8, T, H), BF16),
            pltpu.VMEM((8, T, H), BF16),
            pltpu.SMEM((HALO,), I32),
            pltpu.SMEM((HALO,), I32),
            pltpu.SMEM((HALO,), I32),
            pltpu.SMEM((2 * NC,), I32),
            pltpu.SMEM((KT, 1, FB), I32),
            DMA((8,)),
            DMA((15,)),
            DMA((16,)),
            DMA((16,)),
        ],
        compiler_params=params(collective_id=0, has_side_effects=True),
    )(values, cot, weights, columns, count, fine_halo, coarse_halo, pair_send, members, tiles)


def rows_out(total, blocks, own_ref, halo_ref):
    def own(c):
        own_ref[pl.ds(c * T, T), :] = jnp.transpose(total[c])

    loop(blocks, own, 4)

    def halo(c):
        halo_ref[pl.ds(c * T, T), :] = jnp.transpose(total[blocks + c]).astype(BF16)

    loop(8, halo, 4)


def coarse_kernel(
    own,
    halo,
    z0,
    dz1,
    weights,
    columns_hbm,
    tiles,
    z1_out,
    dm_out,
    piece_out,
    update_out,
    buf,
    ext,
    gates,
    total,
    columns,
    tile_sem,
    index_sem,
):
    index = pltpu.make_async_copy(columns_hbm, columns, index_sem)
    index.start()
    for copy in tile_copies(tiles, buf, tile_sem, 5):
        copy.start()
    ext[pl.ds(0, CB)] = own[...]
    ext[pl.ds(CB, 8)] = halo[...]
    total[...] = jnp.zeros_like(total)
    index.wait()

    def level(i):
        wait_tiles(tiles, buf, tile_sem, i, 4)
        parts = []
        for q in range(4):
            b = i * 4 + q
            parts.append(block_row(buf, columns, ext, b))
        summed = jnp.concatenate(parts, axis=0)
        sigma = jax.nn.sigmoid(summed)
        gate = (summed * sigma).astype(BF16)
        at = pl.ds(i * QUAD, QUAD)
        gates[at, :] = gate
        z1_out[at, :] = (z0[at, :].astype(F32) + dot(gate, weights[3])).astype(BF16)
        slope = sigma * (1.0 + summed * (1.0 - sigma))
        grads = (dot(dz1[at, :], weights[3], NT) * slope).astype(BF16)
        for q in range(4):
            b = i * 4 + q
            grads_t = jnp.transpose(grads[q * T : (q + 1) * T, :])
            spread_row(buf, columns, grads_t, b, total)

    loop(CB // 4, level)
    rows_out(total, CB, dm_out, piece_out)
    update_out[...] = dot(gates[...], dz1[...], TN)


def coarse_level(own, halo, z0, dz1, weights, columns, tiles):
    return pl.pallas_call(
        coarse_kernel,
        name="coarse_level",
        out_shape=[
            shape((NC, H), BF16),
            shape((NC, H), F32),
            shape((HALO, H), BF16),
            shape((H, H), F32),
        ],
        in_specs=[VMEM, VMEM, VMEM, VMEM, VMEM, ANY, ANY],
        out_specs=[VMEM] * 4,
        scratch_shapes=[
            pltpu.VMEM((CB, KT, T, T), BF16),
            pltpu.VMEM((CB + 8, T, H), BF16),
            pltpu.VMEM((NC, H), BF16),
            pltpu.VMEM((CB + 8, T, H), F32),
            pltpu.SMEM((KT, 1, CB), I32),
            DMA((5,)),
            DMA,
        ],
        compiler_params=params(),
    )(own, halo, z0, dz1, weights, columns, tiles)


def loads(pairs, sem):
    return [pltpu.make_async_copy(src, dst, sem.at[i]) for i, (src, dst) in enumerate(pairs)]


def lane_row(index):
    return jnp.concatenate([index[0, j : j + 1, :] for j in range(4)], axis=1)


def returned_rows(named, arrived, base, count):
    row = lax.broadcasted_iota(I32, (count, HALO), 0)
    chosen = jnp.where(jnp.broadcast_to(named - base, (count, HALO)) == row, 1.0, 0.0).astype(BF16)
    return dot(chosen, arrived)


WIDE = 512
ROWS = 48


def placed(rows, numbers):
    high, low = rows // T, rows % T
    at = jnp.broadcast_to(high, (ROWS, WIDE)) == lax.broadcasted_iota(I32, (ROWS, WIDE), 0)
    parts = [
        jnp.where(at, jnp.broadcast_to(part.astype(F32), (ROWS, WIDE)), 0.0).astype(BF16)
        for part in (numbers // 64, numbers % 64)
    ]
    lanes = jnp.where(
        jnp.broadcast_to(low, (T, WIDE)) == lax.broadcasted_iota(I32, (T, WIDE), 0), 1.0, 0.0
    ).astype(BF16)
    return dot(jnp.concatenate(parts, axis=0), lanes, NT)


def whole(tables):
    return (tables[:ROWS] * 64.0 + tables[ROWS:]).astype(I32)


def sources(members, pair_send, live):
    nowhere = ROWS * T - 1
    cells = jnp.zeros((2 * ROWS, T), F32)
    for j in range(2):
        for k in range(NC // WIDE):
            cell = lax.broadcasted_iota(I32, (1, WIDE), 1) + k * WIDE
            row = members[0, j : j + 1, k * WIDE : (k + 1) * WIDE]
            cells = cells + placed(jnp.where(cell < live, row, nowhere), cell + 1)
    slots = jnp.zeros((2 * ROWS, T), F32)
    sent = lane_row(pair_send)
    for k in range(HALO // WIDE):
        slot = lax.broadcasted_iota(I32, (1, WIDE), 1) + (NC + k * WIDE)
        slots = slots + placed(sent[:, k * WIDE : (k + 1) * WIDE], slot + 1)
    cells, slots = whole(cells), whole(slots)
    found = jnp.where(cells > 0, cells, jnp.where(slots > 0, slots, NC + HALO + 1)) - 1
    return jnp.minimum(found, NC + HALO)


def gather_block(index, block, source, target, first, width=2, shift=0):
    for g in range(T // UNROLL):
        rows = [
            source[pl.ds(index[block, g * UNROLL + u] * 2 + shift, width), :]
            for u in range(UNROLL)
        ]
        for u in range(UNROLL):
            target[pl.ds((first + g * UNROLL + u) * width, width), :] = rows[u]


def coarse_back_kernel(
    n,
    weights,
    count,
    coarse_halo,
    pair_send,
    members,
    pieces,
    dm,
    z0_hbm,
    dz1_hbm,
    z1_hbm,
    h1_hbm,
    cot_hbm,
    gate_hbm,
    slope_hbm,
    result_out,
    low_out,
    grads_out,
    message_out,
    update_out,
    arrived,
    rows,
    z0,
    dz1,
    z1,
    h1,
    cot,
    gate,
    slope,
    cells,
    stage,
    send_out,
    recv_out,
    send_away,
    recv_away,
    table,
    source,
    load_sem,
    index_sem,
    send_sem,
    recv_sem,
):
    me = lax.axis_index("dom")
    barrier = greet(me, n)
    early = loads([(dm, rows), (z0_hbm, z0), (dz1_hbm, dz1), (z1_hbm, z1)], load_sem)
    later = loads(
        [(h1_hbm, h1), (cot_hbm, cot), (gate_hbm, gate), (slope_hbm, slope)],
        load_sem.at[pl.ds(4, 4)],
    )
    for copy in early + later:
        copy.start()
    targets = [neighbour(me, n, -offset) for offset in OFFSETS]
    pl.semaphore_wait(barrier, 4)
    back = [
        remote(
            pieces.at[pl.ds(j * SEND, SEND)],
            arrived.at[pl.ds(j * SEND, SEND)],
            send_sem.at[j],
            recv_sem.at[j],
            targets[j],
        )
        for j in range(4)
    ]
    for copy in back:
        copy.start()
    table[...] = sources(members, pair_send, count[0])
    index = pltpu.make_async_copy(table, source, index_sem)
    index.start()
    cells[pl.ds(2 * (NC + HALO), 16), :] = jnp.zeros((16, H), F32)
    message_out[...] = jnp.zeros_like(message_out)
    update_out[...] = jnp.zeros_like(update_out)
    named = lane_row(coarse_halo)
    for copy in early:
        copy.wait()

    def place(i):
        cells[pl.ds(i * 2 * QUAD, QUAD, stride=2), :] = z1[pl.ds(i * QUAD, QUAD), :].astype(F32)

    loop(NC // QUAD, place)

    def exchange_away(shift, sent, received, first):
        copies = []
        for j in range(4):
            loop(
                2,
                lambda t: gather_block(source, FB + 2 * j + t, cells, stage, t * T, 1, shift),
            )
            sent[j] = stage[:SEND, :].astype(BF16)
            copy = remote(
                sent.at[j],
                received.at[j],
                send_sem.at[first + j],
                recv_sem.at[first + j],
                targets[j],
            )
            copy.start()
            copies.append(copy)
        return copies

    index.wait()
    away_out = exchange_away(0, send_out, recv_out, 8)
    for copy in back:
        copy.wait()

    def retract(i):
        at = pl.ds(i * QUAD, QUAD)
        parts = [
            rows[pl.ds(i * QUAD + q * SEND, SEND), :]
            + returned_rows(named, arrived[...], i * QUAD + q * SEND, SEND)
            for q in range(2)
        ]
        low = jnp.concatenate(parts, axis=0).astype(BF16)
        message_out[...] += dot(z0[at, :], low, TN)
        cells[pl.ds(i * 2 * QUAD + 1, QUAD, stride=2), :] = dz1[at, :].astype(F32) + dot(
            low, weights[2], NT
        )

    loop(NC // QUAD, retract)
    away = exchange_away(1, send_away, recv_away, 4)
    for copy in later:
        copy.wait()
    for shift, copies, received in ((0, away_out, recv_out), (1, away, recv_away)):
        for j in range(4):
            copies[j].wait()
            cells[pl.ds(2 * (NC + j * SEND) + shift, SEND, stride=2), :] = received[j].astype(F32)

    def lift(i):
        loop(4, lambda q: gather_block(source, i * 4 + q, cells, stage, q * T))
        at = pl.ds(i * QUAD, QUAD)
        result_out[at, :] = (
            h1[at, :].astype(F32) + stage[pl.ds(0, QUAD, stride=2), :]
        ).astype(BF16)
        low = (cot[at, :].astype(F32) + stage[pl.ds(1, QUAD, stride=2), :]).astype(BF16)
        low_out[at, :] = low
        update_out[...] += dot(gate[at, :], low, TN)
        grads_out[at, :] = (dot(low, weights[1], NT) * slope[at, :].astype(F32)).astype(BF16)

    loop(NF // QUAD, lift)


def coarse_back(
    n, number, weights, count, coarse_halo, pair_send, members, pieces, dm, z0, dz1, z1, h1, cot, gate, slope
):
    return pl.pallas_call(
        functools.partial(coarse_back_kernel, n),
        name="coarse_back",
        out_shape=[
            shape((NF, H), BF16),
            shape((NF, H), BF16),
            shape((NF, H), BF16),
            shape((H, H), F32),
            shape((H, H), F32),
        ],
        in_specs=[VMEM, SMEM, VMEM, VMEM, VMEM] + [ANY] * 9,
        out_specs=[VMEM] * 5,
        scratch_shapes=[
            pltpu.VMEM((HALO, H), BF16),
            pltpu.VMEM((NC, H), F32),
            pltpu.VMEM((NC, H), BF16),
            pltpu.VMEM((NC, H), BF16),
            pltpu.VMEM((NC, H), BF16),
            pltpu.VMEM((NF, H), BF16),
            pltpu.VMEM((NF, H), BF16),
            pltpu.VMEM((NF, H), BF16),
            pltpu.VMEM((NF, H), BF16),
            pltpu.VMEM((2 * (NC + HALO) + 16, H), F32),
            pltpu.VMEM((2 * QUAD, H), F32),
            pltpu.VMEM((4, SEND, H), BF16),
            pltpu.VMEM((4, SEND, H), BF16),
            pltpu.VMEM((4, SEND, H), BF16),
            pltpu.VMEM((4, SEND, H), BF16),
            pltpu.VMEM((ROWS, T), I32),
            pltpu.SMEM((ROWS, T), I32),
            DMA((8,)),
            DMA,
            DMA((12,)),
            DMA((12,)),
        ],
        compiler_params=params(collective_id=number, has_side_effects=True),
    )(weights, count, coarse_halo, pair_send, members, pieces, dm, z0, dz1, z1, h1, cot, gate, slope)


def fine_kernel(
    grads,
    columns_hbm,
    tiles,
    result,
    dm_out,
    piece_out,
    result_out,
    buf,
    total,
    held,
    columns,
    index_sem,
    result_sem,
    tile_sem,
):
    index = pltpu.make_async_copy(columns_hbm, columns, index_sem)
    index.start()
    for copy in tile_copies(tiles, buf, tile_sem, 8):
        copy.start()
    taken = pltpu.make_async_copy(result, held, result_sem.at[0])
    taken.start()
    total[...] = jnp.zeros_like(total)
    index.wait()

    def level(i):
        wait_tiles(tiles, buf, tile_sem, i, 4)
        for q in range(4):
            b = i * 4 + q
            spread_row(buf, columns, jnp.transpose(grads[pl.ds(b * T, T), :]), b, total)

    loop(4, level)
    taken.wait()
    passed = pltpu.make_async_copy(held, result_out, result_sem.at[1])
    passed.start()
    loop(4, lambda i: level(i + 4))
    rows_out(total, FB, dm_out, piece_out)
    passed.wait()


def fine_spread(grads, columns, tiles, result):
    return pl.pallas_call(
        fine_kernel,
        name="fine_spread",
        out_shape=[shape((NF, H), F32), shape((HALO, H), BF16), shape((NF, H), BF16)],
        in_specs=[VMEM, ANY, ANY, ANY],
        out_specs=[VMEM, VMEM, ANY],
        scratch_shapes=[
            pltpu.VMEM((FB, KT, T, T), BF16),
            pltpu.VMEM((FB + 8, T, H), F32),
            pltpu.VMEM((NF, H), BF16),
            pltpu.SMEM((KT, 1, FB), I32),
            DMA,
            DMA((2,)),
            DMA((8,)),
        ],
        compiler_params=params(),
    )(grads, columns, tiles, result)


NEAR = 8
FAR = 16


def scatter_near(grads, near, send, recv, rank, close):
    size = near.shape[1]
    copies = [
        remote(
            grads.at[pl.ds((rank + s + 1) % NEAR * size, size)],
            near.at[s],
            send.at[s],
            recv.at[s],
            close[s],
        )
        for s in range(NEAR - 1)
    ]
    for copy in copies:
        copy.start()
    return copies


def share_far(copies, grads, near, part, far, send, recv, rank, group, distant):
    for copy in copies:
        copy.wait()
    size = near.shape[1]
    summed = grads[pl.ds(rank * size, size), :]
    for s in range(NEAR - 1):
        summed = summed + near[s]
    part[...] = summed
    far[group] = summed
    copies = [
        remote(part, far.at[group], send.at[s], recv.at[s], distant[s]) for s in range(FAR - 1)
    ]
    for copy in copies:
        copy.start()
    return copies


def gather_near(copies, far, total, send, recv, rank, close):
    for copy in copies:
        copy.wait()
    size = far.shape[1]
    summed = far[0]
    for s in range(1, FAR):
        summed = summed + far[s]
    mine = pl.ds(rank * size, size)
    total[mine, :] = summed
    copies = [
        remote(total.at[mine], total.at[mine], send.at[s], recv.at[s], close[s])
        for s in range(NEAR - 1)
    ]
    for copy in copies:
        copy.start()
    return copies


def fine_back_kernel(
    n,
    weights,
    fine_halo,
    u0,
    m1,
    u1,
    pieces,
    dm,
    values_hbm,
    low_hbm,
    grad_out,
    total_out,
    arrived,
    rows,
    values,
    low,
    messages,
    first,
    first_near,
    first_part,
    first_far,
    first_total,
    last,
    last_near,
    last_part,
    last_far,
    last_total,
    load_sem,
    send_sem,
    recv_sem,
    near_send,
    near_recv,
    far_send,
    far_recv,
    all_send,
    all_recv,
):
    me = lax.axis_index("dom")
    group, rank = me // NEAR, me % NEAR
    close = [group * NEAR + (rank + s) % NEAR for s in range(1, NEAR)]
    distant = [((group + s) % FAR) * NEAR + rank for s in range(1, FAR)]
    barrier = greet(me, n)
    for target in close + distant:
        pl.semaphore_signal(barrier, inc=1, device_id=(target,), device_id_type=MESH)
    copies = loads([(dm, rows), (values_hbm, values), (low_hbm, low)], load_sem)
    for copy in copies:
        copy.start()
    for i, ref in enumerate((u0, m1, u1)):
        first[pl.ds(i * H, H), :] = ref[...]
    last[...] = jnp.zeros_like(last)
    named = lane_row(fine_halo)
    pl.semaphore_wait(barrier, 4 + NEAR - 1 + FAR - 1)
    back = [
        remote(
            pieces.at[pl.ds(j * SEND, SEND)],
            arrived.at[pl.ds(j * SEND, SEND)],
            send_sem.at[j],
            recv_sem.at[j],
            neighbour(me, n, -OFFSETS[j]),
        )
        for j in range(4)
    ]
    for copy in back:
        copy.start()
    near1 = scatter_near(first, first_near, near_send.at[0], near_recv.at[0], rank, close)
    for copy in copies + back:
        copy.wait()

    def retract(i):
        at = pl.ds(i * QUAD, QUAD)
        parts = [
            rows[pl.ds(i * QUAD + q * SEND, SEND), :]
            + returned_rows(named, arrived[...], i * QUAD + q * SEND, SEND)
            for q in range(2)
        ]
        part = jnp.concatenate(parts, axis=0).astype(BF16)
        last[...] += dot(values[at, :], part, TN)
        messages[at, :] = part

    def grads(i):
        at = pl.ds(i * QUAD, QUAD)
        grad_out[at, :] = (low[at, :].astype(F32) + dot(messages[at, :], weights[0], NT)).astype(BF16)

    loop(4, retract)
    far1 = share_far(
        near1, first, first_near, first_part, first_far, far_send.at[0], far_recv.at[0], rank, group, distant
    )
    loop(4, lambda i: retract(i + 4))
    near2 = scatter_near(last, last_near, near_send.at[1], near_recv.at[1], rank, close)
    loop(4, grads)
    all1 = gather_near(far1, first_far, first_total, all_send.at[0], all_recv.at[0], rank, close)
    far2 = share_far(
        near2, last, last_near, last_part, last_far, far_send.at[1], far_recv.at[1], rank, group, distant
    )
    loop(4, lambda i: grads(i + 4))
    all2 = gather_near(far2, last_far, last_total, all_send.at[1], all_recv.at[1], rank, close)
    for copy in all1:
        copy.wait()
    total_out[pl.ds(1, 3)] = first_total[...].reshape(3, H, H)
    for copy in all2:
        copy.wait()
    total_out[0] = last_total[...]


def fine_back(n, number, weights, fine_halo, u0, m1, u1, pieces, dm, values, low):
    one, two = 3 * H // NEAR, H // NEAR
    sums = []
    for count, size in ((3 * H, one), (H, two)):
        sums += [
            pltpu.VMEM((count, H), F32),
            pltpu.VMEM((NEAR - 1, size, H), F32),
            pltpu.VMEM((size, H), F32),
            pltpu.VMEM((FAR, size, H), F32),
            pltpu.VMEM((count, H), F32),
        ]
    return pl.pallas_call(
        functools.partial(fine_back_kernel, n),
        name="fine_back",
        out_shape=[shape((NF, H), BF16), shape((4, H, H), F32)],
        in_specs=[VMEM] * 5 + [ANY] * 4,
        out_specs=[VMEM] * 2,
        scratch_shapes=[
            pltpu.VMEM((HALO, H), BF16),
            pltpu.VMEM((NF, H), F32),
            pltpu.VMEM((NF, H), BF16),
            pltpu.VMEM((NF, H), BF16),
            pltpu.VMEM((NF, H), BF16),
        ]
        + sums
        + [
            DMA((3,)),
            DMA((4,)),
            DMA((4,)),
            DMA((2, NEAR - 1)),
            DMA((2, NEAR - 1)),
            DMA((2, FAR - 1)),
            DMA((2, FAR - 1)),
            DMA((2, NEAR - 1)),
            DMA((2, NEAR - 1)),
        ],
        compiler_params=params(collective_id=number, has_side_effects=True),
    )(weights, fine_halo, u0, m1, u1, pieces, dm, values, low)


def finish_kernel(grad, totals, grad_out, totals_out):
    grad_out[...] = grad[...]
    totals_out[...] = totals[...]


def finish(grad, totals):
    return pl.pallas_call(
        finish_kernel,
        name="finish",
        out_shape=[shape(grad.shape, grad.dtype), shape(totals.shape, totals.dtype)],
        in_specs=[VMEM] * 2,
        out_specs=[VMEM] * 2,
        compiler_params=params(),
    )(grad, totals)


def per_device(
    n,
    features,
    cotangent,
    weights,
    fine_tiles,
    fine_columns,
    fine_halo,
    coarse_tiles,
    coarse_columns,
    coarse_halo,
    pair_send,
    members,
    coarse_count,
):
    fine_cols = jnp.transpose(fine_columns, (2, 0, 1))
    coarse_cols = jnp.transpose(coarse_columns, (2, 0, 1))
    h1, gate, slope, own, halo, z0, dz1 = forward(
        n,
        features,
        cotangent,
        weights,
        fine_cols,
        coarse_count,
        fine_halo,
        coarse_halo,
        pair_send,
        members,
        fine_tiles,
    )
    z1, dm1, piece1, update1 = coarse_level(own, halo, z0, dz1, weights, coarse_cols, coarse_tiles)
    result, low, grads, message1, update0 = coarse_back(
        n,
        1,
        weights,
        coarse_count,
        coarse_halo,
        pair_send,
        members,
        piece1,
        dm1,
        z0,
        dz1,
        z1,
        h1,
        cotangent,
        gate,
        slope,
    )
    dm0, piece0, result = fine_spread(grads, fine_cols, fine_tiles, result)
    grad_features, totals = fine_back(
        n, 2, weights, fine_halo, update0, message1, update1, piece0, dm0, features, low
    )
    grad_features, totals = finish(grad_features, totals)
    return result, grad_features, totals


def solution(mesh):
    n = mesh.shape["dom"]
    placed = (
        P("dom", None),
        P("dom", None),
        P(),
        P("dom", None, None, None),
        P("dom", None, None),
        P("dom", None, None),
        P("dom", None, None, None),
        P("dom", None, None),
        P("dom", None, None),
        P("dom", None, None),
        P("dom", None, None),
        P("dom"),
    )
    return jax.shard_map(
        functools.partial(per_device, n),
        mesh=mesh,
        in_specs=placed,
        out_specs=(P("dom", None), P("dom", None), P()),
        check_vma=False,
    )
```

time: 158 us -> 129 us (0.82)
  Pallas kernels: 147 us -> 128 us
  local copies, waits for them, and re-layouts: 9.57 us -> 0 us
    pallas_call x7 -> x4, Pallas kernels: 93.4 us -> 74.5 us  [the longest x1 33.9 us: fine_back(): pl.pallas_call(functools.partial(fine_back_kernel, n), name='fine_back',...]
    unnamed x23 -> x0, local copies, waits for them, and re-layouts: 8.21 us -> none
where the time goes in v2:
time: 129 us
  Pallas kernels  128 us (99%)
  between operations  1.32 us (1%)
    pallas_call x1, Pallas kernels, forward(): pl.pallas_call(functools.partial(forward_kernel, n), name='forward', out_...  41.8 us
    pallas_call x1, Pallas kernels, fine_back(): pl.pallas_call(functools.partial(fine_back_kernel, n), name='fine_back',...  33.9 us
    pallas_call x1, Pallas kernels, coarse_back(): pl.pallas_call(functools.partial(coarse_back_kernel, n), name='coarse_bac...  26.7 us
    pallas_call x1, Pallas kernels, fine_spread(): pl.pallas_call(fine_kernel, name='fine_spread', out_shape=[shape((NF, H),...  11.5 us
    pallas_call x1, Pallas kernels, coarse_level(): pl.pallas_call(coarse_kernel, name='coarse_level', out_shape=[shape((NC,...  11.3 us

profile of v2, /device:TPU:1, one launch (start us, length us, event | category | flops | bytes accessed | tf_op | source)
XLA Modules:
  0.0 128.9 jit_solution(3771996741124773700)
XLA Ops:
  1.3 41.8 %forward.1 = (bf16[4096,128]{1,0:T(8,128)(2,1)}, bf16[4096,128]{1,0:T(8,128)(2,1)}, bf16[4096,128]{1,0:T(8,128)(2,1)}, bf16[20,128,128]{2,1,0:T(8,128)(2,1)}, bf...) custom-call(bf16[4096,128]{1,0:T(8,128)(2,1)} %values_hbm.1, ...), custom_call_target="tpu_custom_call" | custom-call | tf_op jit(solution)/shard_map/forward/pallas_call | solution.py:298
  43.1 11.3 %coarse_level.1 = (bf16[2560,128]{1,0:T(8,128)(2,1)}, f32[2560,128]{1,0:T(8,128)}, bf16[1024,128]{1,0:T(8,128)(2,1)}, f32[128,128]{1,0:T(8,128)}) custom-call(bf16[20,128,128]{2,1,0:T(8,128)(2,1)} %get-tuple-element.26.own, bf16[8,128,128]{2,1,0:T(8,128)(2,1)} %get-tuple-element.27.halo, bf16[2560,128]{1,0:T(8,128)(2,1)} %get-tuple-element.28.z0.z0_hbm, ...), custom_call_target="tpu_custom_call" | custom-call | tf_op jit(solution)/shard_map/coarse_level/pallas_call | solution.py:406
  54.3 26.7 %coarse_back.1 = (bf16[4096,128]{1,0:T(8,128)(2,1)}, bf16[4096,128]{1,0:T(8,128)(2,1)}, bf16[4096,128]{1,0:T(8,128)(2,1)}, f32[128,128]{1,0:T(8,128)}, f32[128,128]{1,0:T(8,128)}) custom-call(bf16[4,128,128]{2,1,0:T(8,128)(2,1)} %weights.7, s32[1]{0:T(128)S(6)} %copy.15.count, s32[1,4,256]{2,1,0:T(4,128)} %coarse_halo.3, s32[1,4,256]{2,1,0:T(4,128)} %pair_send.3, ...), custom_call_target="tpu_custom_call" | custom-call | tf_op jit(solution)/shard_map/coarse_back/pallas_call | solution.py:637
  81.1 11.5 %fine_spread.1 = (f32[4096,128]{1,0:T(8,128)}, bf16[1024,128]{1,0:T(8,128)(2,1)}, bf16[4096,128]{1,0:T(8,128)(2,1)}) custom-call(bf16[4096,128]{1,0:T(8,128)(2,1)} %get-tuple-element.36.grads, s32[12,1,32]{2,1,0:T(1,128)} %bitcast.3, bf16[32,12,128,128]{3,2,1,0:T(8,128)(2,1)} %tiles.5, bf16[4096,128]{1,0:T(8,128)(2,1)} %get-tuple-element.37.result), custom_call_target="tpu_custom_call" | custom-call | tf_op jit(solution)/shard_map/fine_spread/pallas_call | solution.py:717
  92.6 33.9 %fine_back.1 = (bf16[4096,128]{1,0:T(8,128)(2,1)}, f32[4,128,128]{2,1,0:T(8,128)}) custom-call(bf16[4,128,128]{2,1,0:T(8,128)(2,1)} %weights.7, s32[1,4,256]{2,1,0:T(4,128)} %fine_halo.3, f32[128,128]{1,0:T(8,128)} %get-tuple-element.39.u0, f32[128,128]{1,0:T(8,128)} %get-tuple-element.40.m1, f32[128,128]{1,0:T(8,128)} %get-tuple-element.41.u1, ...), custom_call_target="tpu_custom_call" | custom-call | tf_op jit(solution)/shard_map/fine_back/pallas_call | solution.py:908
  126.5 2.4 %finish.1 = (bf16[4096,128]{1,0:T(8,128)(2,1)}, f32[4,128,128]{2,1,0:T(8,128)}) custom-call(bf16[4096,128]{1,0:T(8,128)(2,1)} %get-tuple-element.45.grad, f32[4,128,128]{2,1,0:T(8,128)} %get-tuple-element.46.totals), custom_call_target="tpu_custom_call" | custom-call | tf_op jit(solution)/shard_map/finish/pallas_call | solution.py:943

commit v3 on v2

v3 whole, which is shorter than its diff:
```python
import functools

import jax
import jax.numpy as jnp
from jax import lax
from jax.experimental import pallas as pl
from jax.experimental.pallas import tpu as pltpu
from jax.sharding import PartitionSpec as P

MESH = pl.DeviceIdType.MESH
OFFSETS = (1, -1, 8, -8)
F32, BF16, I32 = jnp.float32, jnp.bfloat16, jnp.int32
VMEM = pl.BlockSpec(memory_space=pltpu.VMEM)
SMEM = pl.BlockSpec(memory_space=pltpu.SMEM)
ANY = pl.BlockSpec(memory_space=pl.ANY)
DMA = pltpu.SemaphoreType.DMA
H = 128
T = 128
KT = 12
FB = 32
CB = 20
NF = FB * T
NC = CB * T
SEND = 256
HALO = 4 * SEND
QUAD = 4 * T
UNROLL = 16
NN = (((1,), (0,)), ((), ()))
NT = (((1,), (1,)), ((), ()))
TN = (((0,), (0,)), ((), ()))


def dot(a, b, how=NN):
    return lax.dot_general(a, b, how, preferred_element_type=F32)


def shape(dims, dtype):
    return jax.ShapeDtypeStruct(dims, dtype)


def params(mib=56, **more):
    return pltpu.CompilerParams(vmem_limit_bytes=mib * 2**20, **more)


def neighbour(me, n, offset):
    return lax.rem(me + (offset + n), n)


def greet(me, n):
    barrier = pltpu.get_barrier_semaphore()
    for offset in OFFSETS:
        pl.semaphore_signal(
            barrier, inc=1, device_id=(neighbour(me, n, offset),), device_id_type=MESH
        )
    return barrier


def remote(src, dst, send_sem, recv_sem, target):
    return pltpu.make_async_remote_copy(
        src_ref=src,
        dst_ref=dst,
        send_sem=send_sem,
        recv_sem=recv_sem,
        device_id=(target,),
        device_id_type=MESH,
    )


def index_copies(pairs, sem):
    copies = []
    for src, dst in pairs:
        width = src.shape[2]
        for j in range(src.shape[1]):
            copies.append((src.at[0, j], dst.at[pl.ds(j * width, width)]))
    return [pltpu.make_async_copy(a, b, sem.at[i]) for i, (a, b) in enumerate(copies)]


def loop(count, body, unroll=1):
    def step(i, carry):
        body(i)
        return carry

    lax.fori_loop(0, count, step, 0, unroll=unroll)


def gather_rows(index, first, source, target, count, step=1, shift=0):
    def body(i):
        base = pl.multiple_of(i * UNROLL, UNROLL)
        rows = [
            source[pl.ds(index[first + base + u] * step + shift, 1), :] for u in range(UNROLL)
        ]
        for u in range(UNROLL):
            target[pl.ds(base + u, 1), :] = rows[u]

    loop(count // UNROLL, body)


def block_row(tiles, columns, blocks, b):
    lhs = jnp.concatenate([tiles[b, k] for k in range(KT)], axis=1)
    rhs = jnp.concatenate([blocks[columns[k, 0, b]] for k in range(KT)], axis=0)
    return dot(lhs, rhs)


def spread_row(tiles, columns, grads_t, b, total):
    for k in range(KT):
        c = columns[k, 0, b]
        total[c] = total[c] + dot(grads_t, tiles[b, k])


def tile_copies(source, buffer, sem, count):
    size = source.shape[0] // count
    return [
        pltpu.make_async_copy(
            source.at[pl.ds(i * size, size)], buffer.at[pl.ds(i * size, size)], sem.at[i]
        )
        for i in range(count)
    ]


def wait_tiles(source, buffer, sem, i, size):
    pltpu.make_async_copy(
        source.at[pl.ds(i * size, size)], buffer.at[pl.ds(i * size, size)], sem.at[i]
    ).wait()


def loads(pairs, sem):
    return [pltpu.make_async_copy(src, dst, sem.at[i]) for i, (src, dst) in enumerate(pairs)]


def forward_kernel(
    n,
    weights,
    count,
    values_hbm,
    cot_hbm,
    columns_hbm,
    fine_halo,
    coarse_halo,
    pair_send,
    members,
    tiles,
    h1_hbm,
    gate_hbm,
    slope_hbm,
    halo_out,
    z0_out,
    z0_halo_out,
    dz1_out,
    values,
    cot,
    h1,
    gates,
    slopes,
    buf,
    ext,
    rows32,
    pairs,
    cells,
    stage,
    send_fine,
    recv_fine,
    send_cot,
    recv_cot,
    send_pair,
    recv_pair,
    send_coarse,
    recv_coarse,
    s_fine,
    s_coarse,
    s_pair,
    s_members,
    columns,
    load_sem,
    store_sem,
    tile_sem,
    index_sem,
    send_sem,
    recv_sem,
):
    me = lax.axis_index("dom")
    barrier = greet(me, n)
    taken = loads([(values_hbm, values), (cot_hbm, cot)], load_sem)
    index = index_copies(
        [(fine_halo, s_fine), (coarse_halo, s_coarse), (pair_send, s_pair), (members, s_members)],
        index_sem,
    )
    index.append(pltpu.make_async_copy(columns_hbm, columns, index_sem.at[14]))
    for copy in taken[:1] + index + taken[1:]:
        copy.start()
    for copy in tile_copies(tiles, buf, tile_sem, 8):
        copy.start()
    taken[0].wait()

    def widen(i):
        at = pl.ds(i * QUAD, QUAD)
        rows32[at, :] = values[at, :].astype(F32)

    loop(NF // QUAD, widen)
    for copy in index:
        copy.wait()
    targets = [neighbour(me, n, offset) for offset in OFFSETS]

    def exchange(index, source, sent, received, first, step=1, shift=0, ready=None):
        copies = []
        for j in range(4):
            gather_rows(index, j * SEND, source, stage, SEND, step, shift)
            sent[j] = stage[...].astype(BF16)
            if ready is not None and j == 0:
                pl.semaphore_wait(ready, 4)
            copy = remote(
                sent.at[j],
                received.at[j],
                send_sem.at[first + j],
                recv_sem.at[first + j],
                targets[j],
            )
            copy.start()
            copies.append(copy)
        return copies

    fine = exchange(s_fine, rows32, send_fine, recv_fine, 0, ready=barrier)

    def project(i):
        at = pl.ds(i * QUAD, QUAD)
        ext[pl.ds(i * 4, 4)] = dot(values[at, :], weights[0]).astype(BF16).reshape(4, T, H)

    loop(NF // QUAD, project)
    taken[1].wait()

    def place_cot(i):
        pairs[pl.ds(i * 2 * QUAD + 1, QUAD, stride=2), :] = cot[pl.ds(i * QUAD, QUAD), :].astype(F32)

    loop(NF // QUAD, place_cot)
    paired_cot = exchange(s_pair, pairs, send_cot, recv_cot, 12, 2, 1)
    for j in range(4):
        fine[j].wait()
        ext[pl.ds(FB + 2 * j, 2)] = dot(recv_fine[j], weights[0]).astype(BF16).reshape(2, T, H)

    def level(i):
        wait_tiles(tiles, buf, tile_sem, i, 4)
        parts = []
        for q in range(4):
            b = i * 4 + q
            parts.append(block_row(buf, columns, ext, b))
        summed = jnp.concatenate(parts, axis=0)
        sigma = jax.nn.sigmoid(summed)
        gate = (summed * sigma).astype(BF16)
        at = pl.ds(i * QUAD, QUAD)
        gates[at, :] = gate
        slopes[at, :] = (sigma * (1.0 + summed * (1.0 - sigma))).astype(BF16)
        out = (values[at, :].astype(F32) + dot(gate, weights[1])).astype(BF16)
        h1[at, :] = out
        pairs[pl.ds(i * 2 * QUAD, QUAD, stride=2), :] = out.astype(F32)

    loop(8, level)
    paired = exchange(s_pair, pairs, send_pair, recv_pair, 4, 2, 0)
    stored = loads([(h1, h1_hbm), (gates, gate_hbm), (slopes, slope_hbm)], store_sem)
    for copy in stored:
        copy.start()
    halo_out[...] = recv_fine[...].reshape(HALO, H)
    for shift, copies, received in ((1, paired_cot, recv_cot), (0, paired, recv_pair)):
        for j in range(4):
            copies[j].wait()
            pairs[pl.ds(2 * (NF + j * SEND) + shift, SEND, stride=2), :] = received[j].astype(F32)

    def pool(i):
        base = pl.multiple_of(i * UNROLL, UNROLL)
        first = [pairs[pl.ds(s_members[base + u] * 2, 2), :] for u in range(UNROLL)]
        second = [pairs[pl.ds(s_members[NC + base + u] * 2, 2), :] for u in range(UNROLL)]
        for u in range(UNROLL):
            cells[pl.ds((base + u) * 2, 2), :] = first[u] + second[u]

    loop(NC // UNROLL, pool)
    live = count[0]

    def pooled(i):
        at = pl.ds(i * QUAD, QUAD)
        row = lax.broadcasted_iota(I32, (QUAD, H), 0) + i * QUAD
        z0 = jnp.where(row < live, cells[pl.ds(i * 2 * QUAD, QUAD, stride=2), :], 0.0).astype(BF16)
        z0_out[at, :] = z0
        rows32[at, :] = z0.astype(F32)

    loop(NC // QUAD, pooled)
    coarse = exchange(s_coarse, rows32, send_coarse, recv_coarse, 8)

    def pooled_cot(i):
        at = pl.ds(i * QUAD, QUAD)
        row = lax.broadcasted_iota(I32, (QUAD, H), 0) + i * QUAD
        dz1_out[at, :] = jnp.where(
            row < live, cells[pl.ds(i * 2 * QUAD + 1, QUAD, stride=2), :], 0.0
        ).astype(BF16)

    loop(NC // QUAD, pooled_cot)
    for copy in stored + coarse:
        copy.wait()
    z0_halo_out[...] = recv_coarse[...].reshape(HALO, H)


def forward(n, weights, count, values, cot, columns, fine_halo, coarse_halo, pair_send, members, tiles):
    return pl.pallas_call(
        functools.partial(forward_kernel, n),
        name="forward",
        out_shape=[
            shape((NF, H), BF16),
            shape((NF, H), BF16),
            shape((NF, H), BF16),
            shape((HALO, H), BF16),
            shape((NC, H), BF16),
            shape((HALO, H), BF16),
            shape((NC, H), BF16),
        ],
        in_specs=[VMEM, SMEM] + [ANY] * 8,
        out_specs=[ANY] * 3 + [VMEM] * 4,
        scratch_shapes=[pltpu.VMEM((NF, H), BF16)] * 5
        + [
            pltpu.VMEM((FB, KT, T, T), BF16),
            pltpu.VMEM((FB + 8, T, H), BF16),
            pltpu.VMEM((NF, H), F32),
            pltpu.VMEM((2 * (NF + HALO), H), F32),
            pltpu.VMEM((2 * NC, H), F32),
            pltpu.VMEM((SEND, H), F32),
        ]
        + [pltpu.VMEM((4, SEND, H), BF16)] * 8
        + [
            pltpu.SMEM((HALO,), I32),
            pltpu.SMEM((HALO,), I32),
            pltpu.SMEM((HALO,), I32),
            pltpu.SMEM((2 * NC,), I32),
            pltpu.SMEM((KT, 1, FB), I32),
            DMA((2,)),
            DMA((3,)),
            DMA((8,)),
            DMA((15,)),
            DMA((16,)),
            DMA((16,)),
        ],
        compiler_params=params(collective_id=0, has_side_effects=True),
    )(weights, count, values, cot, columns, fine_halo, coarse_halo, pair_send, members, tiles)


def rows_out(total, blocks, own_values, halo_values, own_ref, halo_ref, message_ref):
    def own(c):
        part = total[c]
        at = pl.ds(c * T, T)
        own_ref[at, :] = jnp.transpose(part)
        message_ref[...] += dot(part.astype(BF16), own_values[at, :])

    def halo(c):
        part = total[blocks + c]
        at = pl.ds(c * T, T)
        halo_ref[at, :] = jnp.transpose(part).astype(BF16)
        message_ref[...] += dot(part.astype(BF16), halo_values[at, :])

    message_ref[...] = jnp.zeros_like(message_ref)
    loop(blocks, own, 4)
    loop(8, halo, 4)
    message_ref[...] = jnp.transpose(message_ref[...])


def coarse_kernel(
    z0,
    z0_halo,
    dz1,
    weights,
    columns_hbm,
    tiles,
    z1_out,
    dm_out,
    piece_out,
    message_out,
    update_out,
    buf,
    ext,
    gates,
    total,
    columns,
    tile_sem,
    index_sem,
):
    index = pltpu.make_async_copy(columns_hbm, columns, index_sem)
    index.start()
    for copy in tile_copies(tiles, buf, tile_sem, 5):
        copy.start()

    def project(i):
        part = z0[pl.ds(i * QUAD, QUAD), :]
        ext[pl.ds(i * 4, 4)] = dot(part, weights[2]).astype(BF16).reshape(4, T, H)

    loop(CB // 4, project)
    ext[pl.ds(CB, 8)] = dot(z0_halo[...], weights[2]).astype(BF16).reshape(8, T, H)
    total[...] = jnp.zeros_like(total)
    index.wait()

    def level(i):
        wait_tiles(tiles, buf, tile_sem, i, 4)
        parts = []
        for q in range(4):
            b = i * 4 + q
            parts.append(block_row(buf, columns, ext, b))
        summed = jnp.concatenate(parts, axis=0)
        sigma = jax.nn.sigmoid(summed)
        gate = (summed * sigma).astype(BF16)
        at = pl.ds(i * QUAD, QUAD)
        gates[at, :] = gate
        z1_out[at, :] = (z0[at, :].astype(F32) + dot(gate, weights[3])).astype(BF16)
        slope = sigma * (1.0 + summed * (1.0 - sigma))
        grads = (dot(dz1[at, :], weights[3], NT) * slope).astype(BF16)
        for q in range(4):
            b = i * 4 + q
            grads_t = jnp.transpose(grads[q * T : (q + 1) * T, :])
            spread_row(buf, columns, grads_t, b, total)

    loop(CB // 4, level)
    rows_out(total, CB, z0, z0_halo, dm_out, piece_out, message_out)
    update_out[...] = dot(gates[...], dz1[...], TN)


def coarse_level(z0, z0_halo, dz1, weights, columns, tiles):
    return pl.pallas_call(
        coarse_kernel,
        name="coarse_level",
        out_shape=[
            shape((NC, H), BF16),
            shape((NC, H), F32),
            shape((HALO, H), BF16),
            shape((H, H), F32),
            shape((H, H), F32),
        ],
        in_specs=[VMEM, VMEM, VMEM, VMEM, ANY, ANY],
        out_specs=[VMEM] * 5,
        scratch_shapes=[
            pltpu.VMEM((CB, KT, T, T), BF16),
            pltpu.VMEM((CB + 8, T, H), BF16),
            pltpu.VMEM((NC, H), BF16),
            pltpu.VMEM((CB + 8, T, H), F32),
            pltpu.SMEM((KT, 1, CB), I32),
            DMA((5,)),
            DMA,
        ],
        compiler_params=params(),
    )(z0, z0_halo, dz1, weights, columns, tiles)


def lane_row(index):
    return jnp.concatenate([index[0, j : j + 1, :] for j in range(4)], axis=1)


def returned_rows(named, arrived, base, count):
    row = lax.broadcasted_iota(I32, (count, HALO), 0)
    chosen = jnp.where(jnp.broadcast_to(named - base, (count, HALO)) == row, 1.0, 0.0).astype(BF16)
    return dot(chosen, arrived)


WIDE = 512
ROWS = 48


def placed(rows, numbers):
    high, low = rows // T, rows % T
    at = jnp.broadcast_to(high, (ROWS, WIDE)) == lax.broadcasted_iota(I32, (ROWS, WIDE), 0)
    parts = [
        jnp.where(at, jnp.broadcast_to(part.astype(F32), (ROWS, WIDE)), 0.0).astype(BF16)
        for part in (numbers // 64, numbers % 64)
    ]
    lanes = jnp.where(
        jnp.broadcast_to(low, (T, WIDE)) == lax.broadcasted_iota(I32, (T, WIDE), 0), 1.0, 0.0
    ).astype(BF16)
    return dot(jnp.concatenate(parts, axis=0), lanes, NT)


def whole(tables):
    return (tables[:ROWS] * 64.0 + tables[ROWS:]).astype(I32)


def sources(members, pair_send, live):
    nowhere = ROWS * T - 1
    cells = jnp.zeros((2 * ROWS, T), F32)
    for j in range(2):
        for k in range(NC // WIDE):
            cell = lax.broadcasted_iota(I32, (1, WIDE), 1) + k * WIDE
            row = members[0, j : j + 1, k * WIDE : (k + 1) * WIDE]
            cells = cells + placed(jnp.where(cell < live, row, nowhere), cell + 1)
    slots = jnp.zeros((2 * ROWS, T), F32)
    sent = lane_row(pair_send)
    for k in range(HALO // WIDE):
        slot = lax.broadcasted_iota(I32, (1, WIDE), 1) + (NC + k * WIDE)
        slots = slots + placed(sent[:, k * WIDE : (k + 1) * WIDE], slot + 1)
    cells, slots = whole(cells), whole(slots)
    found = jnp.where(cells > 0, cells, jnp.where(slots > 0, slots, NC + HALO + 1)) - 1
    return jnp.minimum(found, NC + HALO)


def gather_block(index, block, source, target, first, width=2, shift=0):
    for g in range(T // UNROLL):
        rows = [
            source[pl.ds(index[block, g * UNROLL + u] * 2 + shift, width), :]
            for u in range(UNROLL)
        ]
        for u in range(UNROLL):
            target[pl.ds((first + g * UNROLL + u) * width, width), :] = rows[u]


NEAR = 8
SIDE = 4
SUM_SEMS = 2 * (NEAR - 1 + SIDE - 1)


class GroupSum:
    def __init__(self, me, grads, near, sides, total, send, recv):
        self.grads, self.near, self.sides, self.total = grads, near, sides, total
        self.send, self.recv = send, recv
        self.rank = me % NEAR
        base = me - self.rank
        self.close = [base + (self.rank + s) % NEAR for s in range(1, NEAR)]
        z, y = me // NEAR % SIDE, me // (NEAR * SIDE)
        self.place = (z, y)
        self.rows = (
            [me + ((z + s) % SIDE - z) * NEAR for s in range(1, SIDE)],
            [me + ((y + s) % SIDE - y) * NEAR * SIDE for s in range(1, SIDE)],
        )
        self.size = near.shape[1]
        self.copies = []

    def greet(self, barrier):
        targets = self.close + self.rows[0] + self.rows[1]
        for target in targets:
            pl.semaphore_signal(barrier, inc=1, device_id=(target,), device_id_type=MESH)
        return len(targets)

    def launch(self, first, moves):
        self.copies = [
            remote(src, dst, self.send.at[first + s], self.recv.at[first + s], target)
            for s, (src, dst, target) in enumerate(moves)
        ]
        for copy in self.copies:
            copy.start()

    def wait(self):
        for copy in self.copies:
            copy.wait()

    def to_near(self):
        size = self.size
        self.launch(
            0,
            [
                (
                    self.grads.at[pl.ds((self.rank + s + 1) % NEAR * size, size)],
                    self.near.at[s],
                    self.close[s],
                )
                for s in range(NEAR - 1)
            ],
        )

    def along(self, side, summed):
        held, place = self.sides[side], self.place[side]
        held[place] = summed
        self.launch(
            NEAR - 1 + side * (SIDE - 1),
            [(held.at[place], held.at[place], target) for target in self.rows[side]],
        )

    def to_z(self):
        self.wait()
        summed = self.grads[pl.ds(self.rank * self.size, self.size), :]
        for s in range(NEAR - 1):
            summed = summed + self.near[s]
        self.along(0, summed)

    def added(self, side):
        self.wait()
        held = self.sides[side]
        return (held[0] + held[1]) + (held[2] + held[3])

    def to_y(self):
        self.along(1, self.added(0))

    def to_all(self):
        mine = pl.ds(self.rank * self.size, self.size)
        self.total[mine, :] = self.added(1)
        self.launch(
            NEAR - 1 + 2 * (SIDE - 1),
            [(self.total.at[mine], self.total.at[mine], target) for target in self.close],
        )


def sum_scratch():
    size = 2 * H // NEAR
    return [
        pltpu.VMEM((2 * H, H), F32),
        pltpu.VMEM((NEAR - 1, size, H), F32),
        pltpu.VMEM((SIDE, size, H), F32),
        pltpu.VMEM((SIDE, size, H), F32),
        pltpu.VMEM((2 * H, H), F32),
        DMA((SUM_SEMS,)),
        DMA((SUM_SEMS,)),
    ]


def coarse_back_kernel(
    n,
    weights,
    count,
    coarse_halo,
    pair_send,
    members,
    m1,
    u1,
    pieces,
    dm,
    dz1_hbm,
    z1_hbm,
    h1_hbm,
    cot_hbm,
    gate_hbm,
    slope_hbm,
    result_hbm,
    low_hbm,
    grads_hbm,
    update_out,
    total_out,
    result_out,
    low_out,
    grads_out,
    arrived,
    rows,
    dz1,
    z1,
    h1,
    cot,
    gate,
    slope,
    cells,
    stage,
    send_out,
    recv_out,
    send_away,
    recv_away,
    table,
    source,
    load_sem,
    store_sem,
    index_sem,
    send_sem,
    recv_sem,
    grads1,
    *sum_refs,
):
    me = lax.axis_index("dom")
    barrier = greet(me, n)
    group = GroupSum(me, grads1, sum_refs[0], sum_refs[1:3], *sum_refs[3:])
    partners = 4 + group.greet(barrier)
    early = loads([(z1_hbm, z1), (dm, rows), (dz1_hbm, dz1)], load_sem)
    later = loads(
        [(h1_hbm, h1), (cot_hbm, cot), (gate_hbm, gate), (slope_hbm, slope)],
        load_sem.at[pl.ds(3, 4)],
    )
    for copy in early + later:
        copy.start()
    targets = [neighbour(me, n, -offset) for offset in OFFSETS]
    grads1[:H, :] = m1[...]
    grads1[H:, :] = u1[...]
    table[...] = sources(members, pair_send, count[0])
    index = pltpu.make_async_copy(table, source, index_sem)
    index.start()
    pl.semaphore_wait(barrier, partners)
    back = [
        remote(
            pieces.at[pl.ds(j * SEND, SEND)],
            arrived.at[pl.ds(j * SEND, SEND)],
            send_sem.at[j],
            recv_sem.at[j],
            targets[j],
        )
        for j in range(4)
    ]
    for copy in back:
        copy.start()
    group.to_near()
    cells[pl.ds(2 * (NC + HALO), 16), :] = jnp.zeros((16, H), F32)
    update_out[...] = jnp.zeros_like(update_out)
    named = lane_row(coarse_halo)
    for copy in early:
        copy.wait()

    def place(i):
        cells[pl.ds(i * 2 * QUAD, QUAD, stride=2), :] = z1[pl.ds(i * QUAD, QUAD), :].astype(F32)

    loop(NC // QUAD, place)

    def exchange_away(shift, sent, received, first):
        copies = []
        for j in range(4):
            loop(
                2,
                lambda t: gather_block(source, FB + 2 * j + t, cells, stage, t * T, 1, shift),
            )
            sent[j] = stage[:SEND, :].astype(BF16)
            copy = remote(
                sent.at[j],
                received.at[j],
                send_sem.at[first + j],
                recv_sem.at[first + j],
                targets[j],
            )
            copy.start()
            copies.append(copy)
        return copies

    index.wait()
    away_out = exchange_away(0, send_out, recv_out, 8)
    group.to_z()
    for copy in back:
        copy.wait()

    def retract(i):
        at = pl.ds(i * QUAD, QUAD)
        parts = [
            rows[pl.ds(i * QUAD + q * SEND, SEND), :]
            + returned_rows(named, arrived[...], i * QUAD + q * SEND, SEND)
            for q in range(2)
        ]
        low = jnp.concatenate(parts, axis=0).astype(BF16)
        cells[pl.ds(i * 2 * QUAD + 1, QUAD, stride=2), :] = dz1[at, :].astype(F32) + dot(
            low, weights[2], NT
        )

    loop(NC // QUAD, retract)
    away = exchange_away(1, send_away, recv_away, 4)
    group.to_y()
    for copy in later:
        copy.wait()
    for shift, copies, received in ((0, away_out, recv_out), (1, away, recv_away)):
        for j in range(4):
            copies[j].wait()
            cells[pl.ds(2 * (NC + j * SEND) + shift, SEND, stride=2), :] = received[j].astype(F32)

    def lift(i):
        loop(4, lambda q: gather_block(source, i * 4 + q, cells, stage, q * T))
        at = pl.ds(i * QUAD, QUAD)
        result_out[at, :] = (
            h1[at, :].astype(F32) + stage[pl.ds(0, QUAD, stride=2), :]
        ).astype(BF16)
        low = (cot[at, :].astype(F32) + stage[pl.ds(1, QUAD, stride=2), :]).astype(BF16)
        low_out[at, :] = low
        update_out[...] += dot(gate[at, :], low, TN)
        grads_out[at, :] = (dot(low, weights[1], NT) * slope[at, :].astype(F32)).astype(BF16)

    group.to_all()
    half = NF // QUAD // 2
    loop(half, lift)
    outs = ((result_out, result_hbm), (low_out, low_hbm), (grads_out, grads_hbm))

    def store(first, sem):
        at = pl.ds(first, NF // 2)
        copies = loads([(src.at[at], dst.at[at]) for src, dst in outs], sem)
        for copy in copies:
            copy.start()
        return copies

    stored = store(0, store_sem.at[pl.ds(0, 3)])
    loop(half, lambda i: lift(i + half))
    stored += store(NF // 2, store_sem.at[pl.ds(3, 3)])
    group.wait()
    total_out[...] = group.total[...]
    for copy in stored:
        copy.wait()


def coarse_back(
    n, number, weights, count, coarse_halo, pair_send, members, m1, u1, pieces, dm, dz1, z1, h1, cot, gate, slope
):
    return pl.pallas_call(
        functools.partial(coarse_back_kernel, n),
        name="coarse_back",
        out_shape=[
            shape((NF, H), BF16),
            shape((NF, H), BF16),
            shape((NF, H), BF16),
            shape((H, H), F32),
            shape((2 * H, H), F32),
        ],
        in_specs=[VMEM, SMEM, VMEM, VMEM, VMEM, VMEM, VMEM] + [ANY] * 8,
        out_specs=[ANY] * 3 + [VMEM] * 2,
        scratch_shapes=[pltpu.VMEM((NF, H), BF16)] * 3
        + [
            pltpu.VMEM((HALO, H), BF16),
            pltpu.VMEM((NC, H), F32),
            pltpu.VMEM((NC, H), BF16),
            pltpu.VMEM((NC, H), BF16),
        ]
        + [pltpu.VMEM((NF, H), BF16)] * 4
        + [
            pltpu.VMEM((2 * (NC + HALO) + 16, H), F32),
            pltpu.VMEM((2 * QUAD, H), F32),
        ]
        + [pltpu.VMEM((4, SEND, H), BF16)] * 4
        + [
            pltpu.VMEM((ROWS, T), I32),
            pltpu.SMEM((ROWS, T), I32),
            DMA((7,)),
            DMA((6,)),
            DMA,
            DMA((12,)),
            DMA((12,)),
        ]
        + sum_scratch(),
        compiler_params=params(collective_id=number, has_side_effects=True),
    )(
        weights,
        count,
        coarse_halo,
        pair_send,
        members,
        m1,
        u1,
        pieces,
        dm,
        dz1,
        z1,
        h1,
        cot,
        gate,
        slope,
    )


def fine_kernel(
    grads,
    values,
    halo,
    columns_hbm,
    tiles,
    result,
    dm_out,
    piece_out,
    message_out,
    result_out,
    buf,
    total,
    held,
    columns,
    index_sem,
    result_sem,
    tile_sem,
):
    index = pltpu.make_async_copy(columns_hbm, columns, index_sem)
    index.start()
    for copy in tile_copies(tiles, buf, tile_sem, 8):
        copy.start()
    taken = pltpu.make_async_copy(result, held, result_sem.at[0])
    taken.start()
    total[...] = jnp.zeros_like(total)
    index.wait()

    def level(i):
        wait_tiles(tiles, buf, tile_sem, i, 4)
        for q in range(4):
            b = i * 4 + q
            spread_row(buf, columns, jnp.transpose(grads[pl.ds(b * T, T), :]), b, total)

    loop(4, level)
    taken.wait()
    passed = pltpu.make_async_copy(held, result_out, result_sem.at[1])
    passed.start()
    loop(4, lambda i: level(i + 4))
    rows_out(total, FB, values, halo, dm_out, piece_out, message_out)
    passed.wait()


def fine_spread(grads, values, halo, columns, tiles, result):
    return pl.pallas_call(
        fine_kernel,
        name="fine_spread",
        out_shape=[
            shape((NF, H), F32),
            shape((HALO, H), BF16),
            shape((H, H), F32),
            shape((NF, H), BF16),
        ],
        in_specs=[VMEM, VMEM, VMEM, ANY, ANY, ANY],
        out_specs=[VMEM, VMEM, VMEM, ANY],
        scratch_shapes=[
            pltpu.VMEM((FB, KT, T, T), BF16),
            pltpu.VMEM((FB + 8, T, H), F32),
            pltpu.VMEM((NF, H), BF16),
            pltpu.SMEM((KT, 1, FB), I32),
            DMA,
            DMA((2,)),
            DMA((8,)),
        ],
        compiler_params=params(),
    )(grads, values, halo, columns, tiles, result)


def fine_back_kernel(
    n,
    weights,
    fine_halo,
    m0,
    u0,
    pieces,
    dm,
    low_hbm,
    grad_out,
    total_out,
    arrived,
    rows,
    low,
    load_sem,
    send_sem,
    recv_sem,
    grads0,
    *sum_refs,
):
    me = lax.axis_index("dom")
    barrier = greet(me, n)
    group = GroupSum(me, grads0, sum_refs[0], sum_refs[1:3], *sum_refs[3:])
    partners = 4 + group.greet(barrier)
    copies = loads([(dm, rows), (low_hbm, low)], load_sem)
    for copy in copies:
        copy.start()
    grads0[:H, :] = m0[...]
    grads0[H:, :] = u0[...]
    named = lane_row(fine_halo)
    pl.semaphore_wait(barrier, partners)
    group.to_near()
    back = [
        remote(
            pieces.at[pl.ds(j * SEND, SEND)],
            arrived.at[pl.ds(j * SEND, SEND)],
            send_sem.at[j],
            recv_sem.at[j],
            neighbour(me, n, -OFFSETS[j]),
        )
        for j in range(4)
    ]
    for copy in back:
        copy.start()
    group.to_z()
    for copy in copies + back:
        copy.wait()

    def retract(i):
        at = pl.ds(i * QUAD, QUAD)
        parts = [
            rows[pl.ds(i * QUAD + q * SEND, SEND), :]
            + returned_rows(named, arrived[...], i * QUAD + q * SEND, SEND)
            for q in range(2)
        ]
        part = jnp.concatenate(parts, axis=0).astype(BF16)
        grad_out[at, :] = (low[at, :].astype(F32) + dot(part, weights[0], NT)).astype(BF16)

    loop(3, retract)
    group.to_y()
    loop(5, lambda i: retract(i + 3))
    group.to_all()
    group.wait()
    total_out[...] = group.total[...]


def fine_back(n, number, weights, fine_halo, m0, u0, pieces, dm, low):
    return pl.pallas_call(
        functools.partial(fine_back_kernel, n),
        name="fine_back",
        out_shape=[shape((NF, H), BF16), shape((2 * H, H), F32)],
        in_specs=[VMEM] * 4 + [ANY] * 3,
        out_specs=[VMEM] * 2,
        scratch_shapes=[
            pltpu.VMEM((HALO, H), BF16),
            pltpu.VMEM((NF, H), F32),
            pltpu.VMEM((NF, H), BF16),
            DMA((2,)),
            DMA((4,)),
            DMA((4,)),
        ]
        + sum_scratch(),
        compiler_params=params(collective_id=number, has_side_effects=True),
    )(weights, fine_halo, m0, u0, pieces, dm, low)


def finish_kernel(grad, fine, coarse, grad_out, totals_out):
    grad_out[...] = grad[...]
    totals_out[pl.ds(0, 2)] = fine[...].reshape(2, H, H)
    totals_out[pl.ds(2, 2)] = coarse[...].reshape(2, H, H)


def finish(grad, fine, coarse):
    return pl.pallas_call(
        finish_kernel,
        name="finish",
        out_shape=[shape(grad.shape, grad.dtype), shape((4, H, H), F32)],
        in_specs=[VMEM] * 3,
        out_specs=[VMEM] * 2,
        compiler_params=params(),
    )(grad, fine, coarse)


def per_device(
    n,
    features,
    cotangent,
    weights,
    fine_tiles,
    fine_columns,
    fine_halo,
    coarse_tiles,
    coarse_columns,
    coarse_halo,
    pair_send,
    members,
    coarse_count,
):
    fine_cols = jnp.transpose(fine_columns, (2, 0, 1))
    coarse_cols = jnp.transpose(coarse_columns, (2, 0, 1))
    h1, gate, slope, halo, z0, z0_halo, dz1 = forward(
        n,
        weights,
        coarse_count,
        features,
        cotangent,
        fine_cols,
        fine_halo,
        coarse_halo,
        pair_send,
        members,
        fine_tiles,
    )
    z1, dm1, piece1, message1, update1 = coarse_level(
        z0, z0_halo, dz1, weights, coarse_cols, coarse_tiles
    )
    result, low, grads, update0, totals1 = coarse_back(
        n,
        1,
        weights,
        coarse_count,
        coarse_halo,
        pair_send,
        members,
        message1,
        update1,
        piece1,
        dm1,
        dz1,
        z1,
        h1,
        cotangent,
        gate,
        slope,
    )
    dm0, piece0, message0, result = fine_spread(
        grads, features, halo, fine_cols, fine_tiles, result
    )
    grad_features, totals0 = fine_back(
        n, 2, weights, fine_halo, message0, update0, piece0, dm0, low
    )
    grad_features, totals = finish(grad_features, totals0, totals1)
    return result, grad_features, totals


def solution(mesh):
    n = mesh.shape["dom"]
    placed = (
        P("dom", None),
        P("dom", None),
        P(),
        P("dom", None, None, None),
        P("dom", None, None),
        P("dom", None, None),
        P("dom", None, None, None),
        P("dom", None, None),
        P("dom", None, None),
        P("dom", None, None),
        P("dom", None, None),
        P("dom"),
    )
    return jax.shard_map(
        functools.partial(per_device, n),
        mesh=mesh,
        in_specs=placed,
        out_specs=(P("dom", None), P("dom", None), P()),
        check_vma=False,
    )
```

time: 129 us -> 120 us (0.930)
  Pallas kernels: 128 us -> 119 us
    pallas_call x1, Pallas kernels: 33.9 us -> 21.5 us  [fine_back(): pl.pallas_call(functools.partial(fine_back_kernel, n), name='fine_back',...]
    pallas_call x1, Pallas kernels: 26.7 us -> 31.4 us  [coarse_back(): pl.pallas_call(functools.partial(coarse_back_kernel, n), name='coarse_bac...]
    pallas_call x1, Pallas kernels: 41.8 us -> 39.6 us  [forward(): pl.pallas_call(functools.partial(forward_kernel, n), name='forward', out_...]
where the time goes in v3:
time: 120 us
  Pallas kernels  119 us (99%)
  between operations  1.32 us (1%)
    pallas_call x1, Pallas kernels, forward(): pl.pallas_call(functools.partial(forward_kernel, n), name='forward', out_...  39.6 us
    pallas_call x1, Pallas kernels, coarse_back(): pl.pallas_call(functools.partial(coarse_back_kernel, n), name='coarse_bac...  31.4 us
    pallas_call x1, Pallas kernels, fine_back(): pl.pallas_call(functools.partial(fine_back_kernel, n), name='fine_back',...  21.5 us
    pallas_call x1, Pallas kernels, fine_spread(): pl.pallas_call(fine_kernel, name='fine_spread', out_shape=[shape((NF, H),...  12.5 us
    pallas_call x1, Pallas kernels, coarse_level(): pl.pallas_call(coarse_kernel, name='coarse_level', out_shape=[shape((NC,...  11.4 us
    pallas_call x1, Pallas kernels, finish(): pl.pallas_call(finish_kernel, name='finish', out_shape=[shape(grad.shape,...  2.42 us

profile of v3, /device:TPU:1, one launch (start us, length us, event | category | flops | bytes accessed | tf_op | source)
XLA Modules:
  0.0 120.1 jit_solution(12003788525934607997)
XLA Ops:
  1.3 39.6 %forward.1 = (bf16[4096,128]{1,0:T(8,128)(2,1)}, bf16[4096,128]{1,0:T(8,128)(2,1)}, bf16[4096,128]{1,0:T(8,128)(2,1)}, bf16[1024,128]{1,0:T(8,128)(2,1)}, bf16[2...) custom-call(bf16[4,128,128]{2,1,0:T(8,128)(2,1)} %weights.7, s32[1]{0:T(128)S(6)} %copy.15.count, ...), custom_call_target="tpu_custom_call" | custom-call | tf_op jit(solution)/shard_map/forward/pallas_call | solution.py:300
  40.9 11.4 %coarse_level.1 = (bf16[2560,128]{1,0:T(8,128)(2,1)}, f32[2560,128]{1,0:T(8,128)}, bf16[1024,128]{1,0:T(8,128)(2,1)}, f32[128,128]{1,0:T(8,128)}, f32[128,128]{1,0:T(8,128)}) custom-call(bf16[2560,128]{1,0:T(8,128)(2,1)} %get-tuple-element.28.z0, bf16[1024,128]{1,0:T(8,128)(2,1)} %get-tuple-element.29.z0_halo, ...), custom_call_target="tpu_custom_call" | custom-call | tf_op jit(solution)/shard_map/coarse_level/pallas_call | solution.py:419
  52.3 31.4 %coarse_back.1 = (bf16[4096,128]{1,0:T(8,128)(2,1)}, bf16[4096,128]{1,0:T(8,128)(2,1)}, bf16[4096,128]{1,0:T(8,128)(2,1)}, f32[128,128]{1,0:T(8,128)}, f32[256,128]{1,0:T(8,128)}) custom-call(bf16[4,128,128]{2,1,0:T(8,128)(2,1)} %weights.7, s32[1]{0:T(128)S(6)} %copy.15.count, s32[1,4,256]{2,1,0:T(4,128)} %coarse_halo.3, s32[1,4,256]{2,1,0:T(4,128)} %pair_send.3, ...), custom_call_target="tpu_custom_call" | custom-call | tf_op jit(solution)/shard_map/coarse_back/pallas_call | solution.py:774
  83.7 12.5 %fine_spread.1 = (f32[4096,128]{1,0:T(8,128)}, bf16[1024,128]{1,0:T(8,128)(2,1)}, f32[128,128]{1,0:T(8,128)}, bf16[4096,128]{1,0:T(8,128)(2,1)}) custom-call(bf16[4096,128]{1,0:T(8,128)(2,1)} %get-tuple-element.39.grads, bf16[4096,128]{1,0:T(8,128)(2,1)} %values.1, bf16[1024,128]{1,0:T(8,128)(2,1)} %get-tuple-element.40.halo, s32[12,1,32]{2,1,0:T(1,128)} %bitcast.3, ...), custom_call_target="tpu_custom_call" | custom-call | tf_op jit(solution)/shard_map/fine_spread/pallas_call | solution.py:873
  96.2 21.5 %fine_back.1 = (bf16[4096,128]{1,0:T(8,128)(2,1)}, f32[256,128]{1,0:T(8,128)}) custom-call(bf16[4,128,128]{2,1,0:T(8,128)(2,1)} %weights.7, s32[1,4,256]{2,1,0:T(4,128)} %fine_halo.3, f32[128,128]{1,0:T(8,128)} %get-tuple-element.43.m0, f32[128,128]{1,0:T(8,128)} %get-tuple-element.44.u0, bf16[1024,128]{1,0:T(8,128)(2,1)} %get-tuple-element.45.pieces, ...), custom_call_target="tpu_custom_call" | custom-call | tf_op jit(solution)/shard_map/fine_back/pallas_call | solution.py:964
  117.7 2.4 %finish.1 = (bf16[4096,128]{1,0:T(8,128)(2,1)}, f32[4,128,128]{2,1,0:T(8,128)}) custom-call(bf16[4096,128]{1,0:T(8,128)(2,1)} %get-tuple-element.48.grad, f32[256,128]{1,0:T(8,128)} %get-tuple-element.49.fine, f32[256,128]{1,0:T(8,128)} %get-tuple-element.50.coarse), custom_call_target="tpu_custom_call" | custom-call | tf_op jit(solution)/shard_map/finish/pallas_call | solution.py:990

commit v4 on v3

--- a/solution.py
+++ b/solution.py
@@ -25,6 +25,8 @@
 HALO = 4 * SEND
 QUAD = 4 * T
 UNROLL = 16
+GATHER = 32
+ORDER = (2, 3, 0, 1)
 NN = (((1,), (0,)), ((), ()))
 NT = (((1,), (1,)), ((), ()))
 TN = (((0,), (0,)), ((), ()))
@@ -85,14 +87,14 @@
 
 def gather_rows(index, first, source, target, count, step=1, shift=0):
     def body(i):
-        base = pl.multiple_of(i * UNROLL, UNROLL)
+        base = pl.multiple_of(i * GATHER, GATHER)
         rows = [
-            source[pl.ds(index[first + base + u] * step + shift, 1), :] for u in range(UNROLL)
+            source[pl.ds(index[first + base + u] * step + shift, 1), :] for u in range(GATHER)
         ]
-        for u in range(UNROLL):
+        for u in range(GATHER):
             target[pl.ds(base + u, 1), :] = rows[u]
 
-    loop(count // UNROLL, body)
+    loop(count // GATHER, body)
 
 
 def block_row(tiles, columns, blocks, b):
@@ -127,10 +129,61 @@
     return [pltpu.make_async_copy(src, dst, sem.at[i]) for i, (src, dst) in enumerate(pairs)]
 
 
+def lane_row(index):
+    return jnp.concatenate([index[0, j : j + 1, :] for j in range(4)], axis=1)
+
+
+def returned_rows(named, arrived, base, count):
+    row = lax.broadcasted_iota(I32, (count, HALO), 0)
+    chosen = jnp.where(jnp.broadcast_to(named - base, (count, HALO)) == row, 1.0, 0.0).astype(BF16)
+    return dot(chosen, arrived)
+
+
+WIDE = 512
+ROWS = 48
+
+
+def placed(rows, numbers):
+    high, low = rows // T, rows % T
+    at = jnp.broadcast_to(high, (ROWS, WIDE)) == lax.broadcasted_iota(I32, (ROWS, WIDE), 0)
+    parts = [
+        jnp.where(at, jnp.broadcast_to(part.astype(F32), (ROWS, WIDE)), 0.0).astype(BF16)
+        for part in (numbers // 64, numbers % 64)
+    ]
+    lanes = jnp.where(
+        jnp.broadcast_to(low, (T, WIDE)) == lax.broadcasted_iota(I32, (T, WIDE), 0), 1.0, 0.0
+    ).astype(BF16)
+    return dot(jnp.concatenate(parts, axis=0), lanes, NT)
+
+
+def whole(tables):
+    return (tables[:ROWS] * 64.0 + tables[ROWS:]).astype(I32)
+
+
+def sources(members, pair_send, live):
+    nowhere = ROWS * T - 1
+    cells = jnp.zeros((2 * ROWS, T), F32)
+    for j in range(2):
+        for k in range(NC // WIDE):
+            cell = lax.broadcasted_iota(I32, (1, WIDE), 1) + k * WIDE
+            row = members[0, j : j + 1, k * WIDE : (k + 1) * WIDE]
+            cells = cells + placed(jnp.where(cell < live, row, nowhere), cell + 1)
+    slots = jnp.zeros((2 * ROWS, T), F32)
+    sent = lane_row(pair_send)
+    for k in range(HALO // WIDE):
+        slot = lax.broadcasted_iota(I32, (1, WIDE), 1) + (NC + k * WIDE)
+        slots = slots + placed(sent[:, k * WIDE : (k + 1) * WIDE], slot + 1)
+    cells, slots = whole(cells), whole(slots)
+    found = jnp.where(cells > 0, cells, jnp.where(slots > 0, slots, NC + HALO + 1)) - 1
+    return jnp.minimum(found, NC + HALO)
+
+
 def forward_kernel(
     n,
     weights,
     count,
+    member_rows,
+    pair_rows,
     values_hbm,
     cot_hbm,
     columns_hbm,
@@ -142,15 +195,18 @@
     h1_hbm,
     gate_hbm,
     slope_hbm,
-    halo_out,
-    z0_out,
-    z0_halo_out,
-    dz1_out,
+    halo_hbm,
+    z0_hbm,
+    z0_halo_hbm,
+    dz1_hbm,
+    table,
     values,
     cot,
     h1,
     gates,
     slopes,
+    z0_rows,
+    dz1_rows,
     buf,
     ext,
     rows32,
@@ -201,11 +257,11 @@
     targets = [neighbour(me, n, offset) for offset in OFFSETS]
 
     def exchange(index, source, sent, received, first, step=1, shift=0, ready=None):
-        copies = []
-        for j in range(4):
+        copies = [None] * 4
+        for j in ORDER:
             gather_rows(index, j * SEND, source, stage, SEND, step, shift)
             sent[j] = stage[...].astype(BF16)
-            if ready is not None and j == 0:
+            if ready is not None and j == ORDER[0]:
                 pl.semaphore_wait(ready, 4)
             copy = remote(
                 sent.at[j],
@@ -215,7 +271,7 @@
                 targets[j],
             )
             copy.start()
-            copies.append(copy)
+            copies[j] = copy
         return copies
 
     fine = exchange(s_fine, rows32, send_fine, recv_fine, 0, ready=barrier)
@@ -232,6 +288,8 @@
 
     loop(NF // QUAD, place_cot)
     paired_cot = exchange(s_pair, pairs, send_cot, recv_cot, 12, 2, 1)
+    table[...] = sources(member_rows, pair_rows, count[0])
+    pairs[pl.ds(2 * NF, HALO, stride=2), :] = jnp.zeros((HALO, H), F32)
     for j in range(4):
         fine[j].wait()
         ext[pl.ds(FB + 2 * j, 2)] = dot(recv_fine[j], weights[0]).astype(BF16).reshape(2, T, H)
@@ -254,46 +312,65 @@
 
     loop(8, level)
     paired = exchange(s_pair, pairs, send_pair, recv_pair, 4, 2, 0)
-    stored = loads([(h1, h1_hbm), (gates, gate_hbm), (slopes, slope_hbm)], store_sem)
+    outs = [(h1, h1_hbm), (gates, gate_hbm), (slopes, slope_hbm), (recv_fine, halo_hbm)]
+    stored = loads(outs, store_sem)
     for copy in stored:
         copy.start()
-    halo_out[...] = recv_fine[...].reshape(HALO, H)
-    for shift, copies, received in ((1, paired_cot, recv_cot), (0, paired, recv_pair)):
-        for j in range(4):
-            copies[j].wait()
-            pairs[pl.ds(2 * (NF + j * SEND) + shift, SEND, stride=2), :] = received[j].astype(F32)
+    for j in range(4):
+        paired_cot[j].wait()
+        pairs[pl.ds(2 * (NF + j * SEND) + 1, SEND, stride=2), :] = recv_cot[j].astype(F32)
 
     def pool(i):
-        base = pl.multiple_of(i * UNROLL, UNROLL)
-        first = [pairs[pl.ds(s_members[base + u] * 2, 2), :] for u in range(UNROLL)]
-        second = [pairs[pl.ds(s_members[NC + base + u] * 2, 2), :] for u in range(UNROLL)]
-        for u in range(UNROLL):
-            cells[pl.ds((base + u) * 2, 2), :] = first[u] + second[u]
-
-    loop(NC // UNROLL, pool)
+        base = pl.multiple_of(i * 2 * GATHER, 2 * GATHER)
+        for half in range(0, 2 * GATHER, GATHER):
+            at = range(half, half + GATHER)
+            first = [pairs[pl.ds(s_members[base + u] * 2, 2), :] for u in at]
+            second = [pairs[pl.ds(s_members[NC + base + u] * 2, 2), :] for u in at]
+            for u in at:
+                cells[pl.ds((base + u) * 2, 2), :] = first[u - half] + second[u - half]
+
+    loop(NC // (2 * GATHER), pool)
     live = count[0]
+    for copy in paired:
+        copy.wait()
+    named = jnp.concatenate([table[FB + t : FB + t + 1, :] for t in range(8)], axis=1)
 
     def pooled(i):
         at = pl.ds(i * QUAD, QUAD)
         row = lax.broadcasted_iota(I32, (QUAD, H), 0) + i * QUAD
-        z0 = jnp.where(row < live, cells[pl.ds(i * 2 * QUAD, QUAD, stride=2), :], 0.0).astype(BF16)
-        z0_out[at, :] = z0
+        received = jnp.concatenate(
+            [
+                returned_rows(named, recv_pair[...].reshape(HALO, H), i * QUAD + q * SEND, SEND)
+                for q in range(2)
+            ],
+            axis=0,
+        )
+        z0 = cells[pl.ds(i * 2 * QUAD, QUAD, stride=2), :] + received
+        z0 = jnp.where(row < live, z0, 0.0).astype(BF16)
+        z0_rows[at, :] = z0
         rows32[at, :] = z0.astype(F32)
 
     loop(NC // QUAD, pooled)
     coarse = exchange(s_coarse, rows32, send_coarse, recv_coarse, 8)
+    stored += loads([(z0_rows, z0_hbm)], store_sem.at[pl.ds(4, 1)])
+    stored[-1].start()
 
     def pooled_cot(i):
         at = pl.ds(i * QUAD, QUAD)
         row = lax.broadcasted_iota(I32, (QUAD, H), 0) + i * QUAD
-        dz1_out[at, :] = jnp.where(
+        dz1_rows[at, :] = jnp.where(
             row < live, cells[pl.ds(i * 2 * QUAD + 1, QUAD, stride=2), :], 0.0
         ).astype(BF16)
 
     loop(NC // QUAD, pooled_cot)
-    for copy in stored + coarse:
+    stored += loads([(dz1_rows, dz1_hbm)], store_sem.at[pl.ds(5, 1)])
+    stored[-1].start()
+    for copy in coarse:
         copy.wait()
-    z0_halo_out[...] = recv_coarse[...].reshape(HALO, H)
+    stored += loads([(recv_coarse, z0_halo_hbm)], store_sem.at[pl.ds(6, 1)])
+    stored[-1].start()
+    for copy in stored:
+        copy.wait()
 
 
 def forward(n, weights, count, values, cot, columns, fine_halo, coarse_halo, pair_send, members, tiles):
@@ -304,14 +381,16 @@
             shape((NF, H), BF16),
             shape((NF, H), BF16),
             shape((NF, H), BF16),
-            shape((HALO, H), BF16),
+            shape((4, SEND, H), BF16),
             shape((NC, H), BF16),
-            shape((HALO, H), BF16),
+            shape((4, SEND, H), BF16),
             shape((NC, H), BF16),
+            shape((ROWS, T), I32),
         ],
-        in_specs=[VMEM, SMEM] + [ANY] * 8,
-        out_specs=[ANY] * 3 + [VMEM] * 4,
+        in_specs=[VMEM, SMEM, VMEM, VMEM] + [ANY] * 8,
+        out_specs=[ANY] * 7 + [VMEM],
         scratch_shapes=[pltpu.VMEM((NF, H), BF16)] * 5
+        + [pltpu.VMEM((NC, H), BF16)] * 2
         + [
             pltpu.VMEM((FB, KT, T, T), BF16),
             pltpu.VMEM((FB + 8, T, H), BF16),
@@ -328,33 +407,53 @@
             pltpu.SMEM((2 * NC,), I32),
             pltpu.SMEM((KT, 1, FB), I32),
             DMA((2,)),
-            DMA((3,)),
+            DMA((7,)),
             DMA((8,)),
             DMA((15,)),
             DMA((16,)),
             DMA((16,)),
         ],
         compiler_params=params(collective_id=0, has_side_effects=True),
-    )(weights, count, values, cot, columns, fine_halo, coarse_halo, pair_send, members, tiles)
-
-
-def rows_out(total, blocks, own_values, halo_values, own_ref, halo_ref, message_ref):
-    def own(c):
+    )(
+        weights,
+        count,
+        members,
+        pair_send,
+        values,
+        cot,
+        columns,
+        fine_halo,
+        coarse_halo,
+        pair_send,
+        members,
+        tiles,
+    )
+
+
+def rows_out(total, blocks, own_values, halo_values, own, own_hbm, sem, halo_ref, message_ref):
+    def place(c):
         part = total[c]
         at = pl.ds(c * T, T)
-        own_ref[at, :] = jnp.transpose(part)
+        own[at, :] = jnp.transpose(part)
         message_ref[...] += dot(part.astype(BF16), own_values[at, :])
 
     def halo(c):
         part = total[blocks + c]
-        at = pl.ds(c * T, T)
-        halo_ref[at, :] = jnp.transpose(part).astype(BF16)
-        message_ref[...] += dot(part.astype(BF16), halo_values[at, :])
+        halo_ref[pl.ds(c * T, T), :] = jnp.transpose(part).astype(BF16)
+        message_ref[...] += dot(part.astype(BF16), halo_values[c // 2, pl.ds(c % 2 * T, T), :])
 
     message_ref[...] = jnp.zeros_like(message_ref)
-    loop(blocks, own, 4)
-    loop(8, halo, 4)
+    quarter = blocks // 4
+    copies = []
+    for part in range(4):
+        loop(quarter, lambda c: place(part * quarter + c), quarter)
+        at = pl.ds(part * quarter * T, quarter * T)
+        copies.append(pltpu.make_async_copy(own.at[at], own_hbm.at[at], sem.at[part]))
+        copies[-1].start()
+    loop(8, halo, 8)
     message_ref[...] = jnp.transpose(message_ref[...])
+    for copy in copies:
+        copy.wait()
 
 
 def coarse_kernel(
@@ -365,10 +464,12 @@
     columns_hbm,
     tiles,
     z1_out,
-    dm_out,
+    dm_hbm,
     piece_out,
     message_out,
     update_out,
+    dm,
+    dm_sem,
     buf,
     ext,
     gates,
@@ -387,7 +488,7 @@
         ext[pl.ds(i * 4, 4)] = dot(part, weights[2]).astype(BF16).reshape(4, T, H)
 
     loop(CB // 4, project)
-    ext[pl.ds(CB, 8)] = dot(z0_halo[...], weights[2]).astype(BF16).reshape(8, T, H)
+    ext[pl.ds(CB, 8)] = dot(z0_halo[...].reshape(HALO, H), weights[2]).astype(BF16).reshape(8, T, H)
     total[...] = jnp.zeros_like(total)
     index.wait()
 
@@ -411,8 +512,8 @@
             spread_row(buf, columns, grads_t, b, total)
 
     loop(CB // 4, level)
-    rows_out(total, CB, z0, z0_halo, dm_out, piece_out, message_out)
     update_out[...] = dot(gates[...], dz1[...], TN)
+    rows_out(total, CB, z0, z0_halo, dm, dm_hbm, dm_sem, piece_out, message_out)
 
 
 def coarse_level(z0, z0_halo, dz1, weights, columns, tiles):
@@ -427,8 +528,10 @@
             shape((H, H), F32),
         ],
         in_specs=[VMEM, VMEM, VMEM, VMEM, ANY, ANY],
-        out_specs=[VMEM] * 5,
+        out_specs=[VMEM, ANY, VMEM, VMEM, VMEM],
         scratch_shapes=[
+            pltpu.VMEM((NC, H), F32),
+            DMA((4,)),
             pltpu.VMEM((CB, KT, T, T), BF16),
             pltpu.VMEM((CB + 8, T, H), BF16),
             pltpu.VMEM((NC, H), BF16),
@@ -439,55 +542,6 @@
         ],
         compiler_params=params(),
     )(z0, z0_halo, dz1, weights, columns, tiles)
-
-
-def lane_row(index):
-    return jnp.concatenate([index[0, j : j + 1, :] for j in range(4)], axis=1)
-
-
-def returned_rows(named, arrived, base, count):
-    row = lax.broadcasted_iota(I32, (count, HALO), 0)
-    chosen = jnp.where(jnp.broadcast_to(named - base, (count, HALO)) == row, 1.0, 0.0).astype(BF16)
-    return dot(chosen, arrived)
-
-
-WIDE = 512
-ROWS = 48
-
-
-def placed(rows, numbers):
-    high, low = rows // T, rows % T
-    at = jnp.broadcast_to(high, (ROWS, WIDE)) == lax.broadcasted_iota(I32, (ROWS, WIDE), 0)
-    parts = [
-        jnp.where(at, jnp.broadcast_to(part.astype(F32), (ROWS, WIDE)), 0.0).astype(BF16)
-        for part in (numbers // 64, numbers % 64)
-    ]
-    lanes = jnp.where(
-        jnp.broadcast_to(low, (T, WIDE)) == lax.broadcasted_iota(I32, (T, WIDE), 0), 1.0, 0.0
-    ).astype(BF16)
-    return dot(jnp.concatenate(parts, axis=0), lanes, NT)
-
-
-def whole(tables):
-    return (tables[:ROWS] * 64.0 + tables[ROWS:]).astype(I32)
-
-
-def sources(members, pair_send, live):
-    nowhere = ROWS * T - 1
-    cells = jnp.zeros((2 * ROWS, T), F32)
-    for j in range(2):
-        for k in range(NC // WIDE):
-            cell = lax.broadcasted_iota(I32, (1, WIDE), 1) + k * WIDE
-            row = members[0, j : j + 1, k * WIDE : (k + 1) * WIDE]
-            cells = cells + placed(jnp.where(cell < live, row, nowhere), cell + 1)
-    slots = jnp.zeros((2 * ROWS, T), F32)
-    sent = lane_row(pair_send)
-    for k in range(HALO // WIDE):
-        slot = lax.broadcasted_iota(I32, (1, WIDE), 1) + (NC + k * WIDE)
-        slots = slots + placed(sent[:, k * WIDE : (k + 1) * WIDE], slot + 1)
-    cells, slots = whole(cells), whole(slots)
-    found = jnp.where(cells > 0, cells, jnp.where(slots > 0, slots, NC + HALO + 1)) - 1
-    return jnp.minimum(found, NC + HALO)
 
 
 def gather_block(index, block, source, target, first, width=2, shift=0):
@@ -601,12 +655,10 @@
 def coarse_back_kernel(
     n,
     weights,
-    count,
     coarse_halo,
-    pair_send,
-    members,
     m1,
     u1,
+    table,
     pieces,
     dm,
     dz1_hbm,
@@ -633,11 +685,12 @@
     slope,
     cells,
     stage,
+    even,
+    odd,
     send_out,
     recv_out,
     send_away,
     recv_away,
-    table,
     source,
     load_sem,
     store_sem,
@@ -661,7 +714,6 @@
     targets = [neighbour(me, n, -offset) for offset in OFFSETS]
     grads1[:H, :] = m1[...]
     grads1[H:, :] = u1[...]
-    table[...] = sources(members, pair_send, count[0])
     index = pltpu.make_async_copy(table, source, index_sem)
     index.start()
     pl.semaphore_wait(barrier, partners)
@@ -673,7 +725,7 @@
             recv_sem.at[j],
             targets[j],
         )
-        for j in range(4)
+        for j in ORDER
     ]
     for copy in back:
         copy.start()
@@ -690,13 +742,13 @@
     loop(NC // QUAD, place)
 
     def exchange_away(shift, sent, received, first):
-        copies = []
-        for j in range(4):
+        copies = [None] * 4
+        for j in ORDER:
             loop(
                 2,
                 lambda t: gather_block(source, FB + 2 * j + t, cells, stage, t * T, 1, shift),
             )
-            sent[j] = stage[:SEND, :].astype(BF16)
+            sent[j] = stage[...].astype(BF16)
             copy = remote(
                 sent.at[j],
                 received.at[j],
@@ -705,7 +757,7 @@
                 targets[j],
             )
             copy.start()
-            copies.append(copy)
+            copies[j] = copy
         return copies
 
     index.wait()
@@ -736,20 +788,24 @@
             copies[j].wait()
             cells[pl.ds(2 * (NC + j * SEND) + shift, SEND, stride=2), :] = received[j].astype(F32)
 
-    def lift(i):
-        loop(4, lambda q: gather_block(source, i * 4 + q, cells, stage, q * T))
-        at = pl.ds(i * QUAD, QUAD)
-        result_out[at, :] = (
-            h1[at, :].astype(F32) + stage[pl.ds(0, QUAD, stride=2), :]
-        ).astype(BF16)
-        low = (cot[at, :].astype(F32) + stage[pl.ds(1, QUAD, stride=2), :]).astype(BF16)
+    def lift(b, lifted):
+        at = pl.ds(b * T, T)
+        result_out[at, :] = (h1[at, :].astype(F32) + lifted[pl.ds(0, T, stride=2), :]).astype(BF16)
+        low = (cot[at, :].astype(F32) + lifted[pl.ds(1, T, stride=2), :]).astype(BF16)
         low_out[at, :] = low
         update_out[...] += dot(gate[at, :], low, TN)
         grads_out[at, :] = (dot(low, weights[1], NT) * slope[at, :].astype(F32)).astype(BF16)
 
+    def lift_two(i):
+        gather_block(source, 2 * i + 1, cells, odd, 0)
+        lift(2 * i, even)
+        gather_block(source, (2 * i + 2) % FB, cells, even, 0)
+        lift(2 * i + 1, odd)
+
     group.to_all()
-    half = NF // QUAD // 2
-    loop(half, lift)
+    gather_block(source, 0, cells, even, 0)
+    half = FB // 4
+    loop(half, lift_two)
     outs = ((result_out, result_hbm), (low_out, low_hbm), (grads_out, grads_hbm))
 
     def store(first, sem):
@@ -760,7 +816,7 @@
         return copies
 
     stored = store(0, store_sem.at[pl.ds(0, 3)])
-    loop(half, lambda i: lift(i + half))
+    loop(half, lambda i: lift_two(i + half))
     stored += store(NF // 2, store_sem.at[pl.ds(3, 3)])
     group.wait()
     total_out[...] = group.total[...]
@@ -769,7 +825,7 @@
 
 
 def coarse_back(
-    n, number, weights, count, coarse_halo, pair_send, members, m1, u1, pieces, dm, dz1, z1, h1, cot, gate, slope
+    n, number, weights, coarse_halo, m1, u1, table, pieces, dm, dz1, z1, h1, cot, gate, slope
 ):
     return pl.pallas_call(
         functools.partial(coarse_back_kernel, n),
@@ -781,7 +837,7 @@
             shape((H, H), F32),
             shape((2 * H, H), F32),
         ],
-        in_specs=[VMEM, SMEM, VMEM, VMEM, VMEM, VMEM, VMEM] + [ANY] * 8,
+        in_specs=[VMEM] * 4 + [ANY] * 9,
         out_specs=[ANY] * 3 + [VMEM] * 2,
         scratch_shapes=[pltpu.VMEM((NF, H), BF16)] * 3
         + [
@@ -793,11 +849,12 @@
         + [pltpu.VMEM((NF, H), BF16)] * 4
         + [
             pltpu.VMEM((2 * (NC + HALO) + 16, H), F32),
-            pltpu.VMEM((2 * QUAD, H), F32),
+            pltpu.VMEM((SEND, H), F32),
+            pltpu.VMEM((2 * T, H), F32),
+            pltpu.VMEM((2 * T, H), F32),
         ]
         + [pltpu.VMEM((4, SEND, H), BF16)] * 4
         + [
-            pltpu.VMEM((ROWS, T), I32),
             pltpu.SMEM((ROWS, T), I32),
             DMA((7,)),
             DMA((6,)),
@@ -809,12 +866,10 @@
         compiler_params=params(collective_id=number, has_side_effects=True),
     )(
         weights,
-        count,
         coarse_halo,
-        pair_send,
-        members,
         m1,
         u1,
+        table,
         pieces,
         dm,
         dz1,
@@ -827,32 +882,41 @@
 
 
 def fine_kernel(
+    grads_hbm,
+    values_hbm,
+    halo_hbm,
+    columns_hbm,
+    tiles,
+    result_in,
+    dm_hbm,
+    piece_out,
+    message_out,
+    result_out,
     grads,
     values,
     halo,
-    columns_hbm,
-    tiles,
     result,
-    dm_out,
-    piece_out,
-    message_out,
-    result_out,
+    dm,
     buf,
     total,
-    held,
     columns,
-    index_sem,
-    result_sem,
+    load_sem,
+    store_sem,
     tile_sem,
 ):
-    index = pltpu.make_async_copy(columns_hbm, columns, index_sem)
-    index.start()
+    first = loads([(columns_hbm, columns), (grads_hbm, grads)], load_sem)
+    for copy in first:
+        copy.start()
     for copy in tile_copies(tiles, buf, tile_sem, 8):
         copy.start()
-    taken = pltpu.make_async_copy(result, held, result_sem.at[0])
-    taken.start()
+    later = loads(
+        [(values_hbm, values), (halo_hbm, halo), (result_in, result)], load_sem.at[pl.ds(2, 3)]
+    )
+    for copy in later:
+        copy.start()
     total[...] = jnp.zeros_like(total)
-    index.wait()
+    for copy in first:
+        copy.wait()
 
     def level(i):
         wait_tiles(tiles, buf, tile_sem, i, 4)
@@ -860,12 +924,13 @@
             b = i * 4 + q
             spread_row(buf, columns, jnp.transpose(grads[pl.ds(b * T, T), :]), b, total)
 
-    loop(4, level)
-    taken.wait()
-    passed = pltpu.make_async_copy(held, result_out, result_sem.at[1])
+    loop(6, level)
+    for copy in later:
+        copy.wait()
+    passed = pltpu.make_async_copy(result, result_out, store_sem.at[4])
     passed.start()
-    loop(4, lambda i: level(i + 4))
-    rows_out(total, FB, values, halo, dm_out, piece_out, message_out)
+    loop(2, lambda i: level(i + 6))
+    rows_out(total, FB, values, halo, dm, dm_hbm, store_sem, piece_out, message_out)
     passed.wait()
 
 
@@ -879,15 +944,19 @@
             shape((H, H), F32),
             shape((NF, H), BF16),
         ],
-        in_specs=[VMEM, VMEM, VMEM, ANY, ANY, ANY],
-        out_specs=[VMEM, VMEM, VMEM, ANY],
+        in_specs=[ANY] * 6,
+        out_specs=[ANY, VMEM, VMEM, ANY],
         scratch_shapes=[
+            pltpu.VMEM((NF, H), BF16),
+            pltpu.VMEM((NF, H), BF16),
+            pltpu.VMEM((4, SEND, H), BF16),
+            pltpu.VMEM((NF, H), BF16),
+            pltpu.VMEM((NF, H), F32),
             pltpu.VMEM((FB, KT, T, T), BF16),
             pltpu.VMEM((FB + 8, T, H), F32),
-            pltpu.VMEM((NF, H), BF16),
             pltpu.SMEM((KT, 1, FB), I32),
-            DMA,
-            DMA((2,)),
+            DMA((5,)),
+            DMA((5,)),
             DMA((8,)),
         ],
         compiler_params=params(),
@@ -934,7 +1003,7 @@
             recv_sem.at[j],
             neighbour(me, n, -OFFSETS[j]),
         )
-        for j in range(4)
+        for j in ORDER
     ]
     for copy in back:
         copy.start()
@@ -1014,7 +1083,7 @@
 ):
     fine_cols = jnp.transpose(fine_columns, (2, 0, 1))
     coarse_cols = jnp.transpose(coarse_columns, (2, 0, 1))
-    h1, gate, slope, halo, z0, z0_halo, dz1 = forward(
+    h1, gate, slope, halo, z0, z0_halo, dz1, table = forward(
         n,
         weights,
         coarse_count,
@@ -1034,12 +1103,10 @@
         n,
         1,
         weights,
-        coarse_count,
         coarse_halo,
-        pair_send,
-        members,
         message1,
         update1,
+        table,
         piece1,
         dm1,
         dz1,

time: 120 us -> 117 us (0.975)
  Pallas kernels: 119 us -> 115 us
    pallas_call x1, Pallas kernels: 39.6 us -> 37.2 us  [forward(): pl.pallas_call(functools.partial(forward_kernel, n), name='forward', out_...]
    pallas_call x1, Pallas kernels: 21.5 us -> 23.9 us  [fine_back(): pl.pallas_call(functools.partial(fine_back_kernel, n), name='fine_back',...]
    pallas_call x1, Pallas kernels: 12.5 us -> 10.7 us  [fine_spread(): pl.pallas_call(fine_kernel, name='fine_spread', out_shape=[shape((NF, H),...]
    pallas_call x1, Pallas kernels: 31.4 us -> 29.8 us  [coarse_back(): pl.pallas_call(functools.partial(coarse_back_kernel, n), name='coarse_bac...]
where the time goes in v4:
time: 117 us
  Pallas kernels  115 us (98%)
  between operations  1.32 us (1%)
    pallas_call x1, Pallas kernels, forward(): pl.pallas_call(functools.partial(forward_kernel, n), name='forward', out_...  37.2 us
    pallas_call x1, Pallas kernels, coarse_back(): pl.pallas_call(functools.partial(coarse_back_kernel, n), name='coarse_bac...  29.8 us
    pallas_call x1, Pallas kernels, fine_back(): pl.pallas_call(functools.partial(fine_back_kernel, n), name='fine_back',...  23.9 us
    pallas_call x1, Pallas kernels, coarse_level(): pl.pallas_call(coarse_kernel, name='coarse_level', out_shape=[shape((NC,...  11.4 us
    pallas_call x1, Pallas kernels, fine_spread(): pl.pallas_call(fine_kernel, name='fine_spread', out_shape=[shape((NF, H),...  10.7 us
    pallas_call x1, Pallas kernels, finish(): pl.pallas_call(finish_kernel, name='finish', out_shape=[shape(grad.shape,...  2.42 us

profile of v4, /device:TPU:1, one launch (start us, length us, event | category | flops | bytes accessed | tf_op | source)
XLA Modules:
  0.0 116.8 jit_solution(5377089055042333314)
XLA Ops:
  1.3 37.2 %forward.1 = (bf16[4096,128]{1,0:T(8,128)(2,1)}, bf16[4096,128]{1,0:T(8,128)(2,1)}, bf16[4096,128]{1,0:T(8,128)(2,1)}, bf16[4,256,128]{2,1,0:T(8,128)(2,1)}, bf1...) custom-call(bf16[4,128,128]{2,1,0:T(8,128)(2,1)} %weights.7, ...), custom_call_target="tpu_custom_call" | custom-call | tf_op jit(solution)/shard_map/forward/pallas_call | solution.py:377
  38.5 11.4 %coarse_level.1 = (bf16[2560,128]{1,0:T(8,128)(2,1)}, f32[2560,128]{1,0:T(8,128)}, bf16[1024,128]{1,0:T(8,128)(2,1)}, f32[128,128]{1,0:T(8,128)}, f32[128,128]{1,0:T(8,128)}) custom-call(bf16[2560,128]{1,0:T(8,128)(2,1)} %get-tuple-element.29.z0, bf16[4,256,128]{2,1,0:T(8,128)(2,1)} %get-tuple-element.30.z0_halo, ...), custom_call_target="tpu_custom_call" | custom-call | tf_op jit(solution)/shard_map/coarse_level/pallas_call | solution.py:520
  49.9 29.8 %coarse_back.1 = (bf16[4096,128]{1,0:T(8,128)(2,1)}, bf16[4096,128]{1,0:T(8,128)(2,1)}, bf16[4096,128]{1,0:T(8,128)(2,1)}, f32[128,128]{1,0:T(8,128)}, f32[256,128]{1,0:T(8,128)}) custom-call(bf16[4,128,128]{2,1,0:T(8,128)(2,1)} %weights.7, s32[1,4,256]{2,1,0:T(4,128)} %coarse_halo.3, f32[128,128]{1,0:T(8,128)} %get-tuple-element.32.m1, ...), custom_call_target="tpu_custom_call" | custom-call | tf_op jit(solution)/shard_map/coarse_back/pallas_call | solution.py:830
  79.7 10.7 %fine_spread.1 = (f32[4096,128]{1,0:T(8,128)}, bf16[1024,128]{1,0:T(8,128)(2,1)}, f32[128,128]{1,0:T(8,128)}, bf16[4096,128]{1,0:T(8,128)(2,1)}) custom-call(bf16[4096,128]{1,0:T(8,128)(2,1)} %get-tuple-element.41.grads_hbm, bf16[4096,128]{1,0:T(8,128)(2,1)} %values_hbm.3, bf16[4,256,128]{2,1,0:T(8,128)(2,1)} %get-tuple-element.42.halo_hbm, ...), custom_call_target="tpu_custom_call" | custom-call | tf_op jit(solution)/shard_map/fine_spread/pallas_call | solution.py:938
  90.4 23.9 %fine_back.1 = (bf16[4096,128]{1,0:T(8,128)(2,1)}, f32[256,128]{1,0:T(8,128)}) custom-call(bf16[4,128,128]{2,1,0:T(8,128)(2,1)} %weights.7, s32[1,4,256]{2,1,0:T(4,128)} %fine_halo.3, f32[128,128]{1,0:T(8,128)} %get-tuple-element.45.m0, f32[128,128]{1,0:T(8,128)} %get-tuple-element.46.u0, bf16[1024,128]{1,0:T(8,128)(2,1)} %get-tuple-element.47.pieces, ...), custom_call_target="tpu_custom_call" | custom-call | tf_op jit(solution)/shard_map/fine_back/pallas_call | solution.py:1033
  114.3 2.4 %finish.1 = (bf16[4096,128]{1,0:T(8,128)(2,1)}, f32[4,128,128]{2,1,0:T(8,128)}) custom-call(bf16[4096,128]{1,0:T(8,128)(2,1)} %get-tuple-element.50.grad, f32[256,128]{1,0:T(8,128)} %get-tuple-element.51.fine, f32[256,128]{1,0:T(8,128)} %get-tuple-element.52.coarse), custom_call_target="tpu_custom_call" | custom-call | tf_op jit(solution)/shard_map/finish/pallas_call | solution.py:1059

commit v5 on v4

--- a/solution.py
+++ b/solution.py
@@ -119,6 +119,23 @@
     ]
 
 
+AHEAD = 2
+
+
+def start_tiles(source, buffer, sem, i, size):
+    pltpu.make_async_copy(
+        source.at[pl.ds(i * size, size)], buffer.at[pl.ds(i * size, size)], sem.at[i]
+    ).start()
+
+
+def next_tiles(source, buffer, sem, i, size):
+    wait_tiles(source, buffer, sem, i, size)
+
+    @pl.when(i + AHEAD < source.shape[0] // size)
+    def _():
+        start_tiles(source, buffer, sem, i + AHEAD, size)
+
+
 def wait_tiles(source, buffer, sem, i, size):
     pltpu.make_async_copy(
         source.at[pl.ds(i * size, size)], buffer.at[pl.ds(i * size, size)], sem.at[i]
@@ -181,9 +198,9 @@
 def forward_kernel(
     n,
     weights,
-    count,
     member_rows,
     pair_rows,
+    count_hbm,
     values_hbm,
     cot_hbm,
     columns_hbm,
@@ -226,6 +243,7 @@
     s_pair,
     s_members,
     columns,
+    count,
     load_sem,
     store_sem,
     tile_sem,
@@ -241,11 +259,13 @@
         index_sem,
     )
     index.append(pltpu.make_async_copy(columns_hbm, columns, index_sem.at[14]))
-    for copy in taken[:1] + index + taken[1:]:
+    index.append(pltpu.make_async_copy(count_hbm, count, index_sem.at[15]))
+    for copy in taken[:1] + index:
         copy.start()
+    taken[0].wait()
+    taken[1].start()
     for copy in tile_copies(tiles, buf, tile_sem, 8):
         copy.start()
-    taken[0].wait()
 
     def widen(i):
         at = pl.ds(i * QUAD, QUAD)
@@ -387,7 +407,7 @@
             shape((NC, H), BF16),
             shape((ROWS, T), I32),
         ],
-        in_specs=[VMEM, SMEM, VMEM, VMEM] + [ANY] * 8,
+        in_specs=[VMEM] * 3 + [ANY] * 9,
         out_specs=[ANY] * 7 + [VMEM],
         scratch_shapes=[pltpu.VMEM((NF, H), BF16)] * 5
         + [pltpu.VMEM((NC, H), BF16)] * 2
@@ -406,19 +426,20 @@
             pltpu.SMEM((HALO,), I32),
             pltpu.SMEM((2 * NC,), I32),
             pltpu.SMEM((KT, 1, FB), I32),
+            pltpu.SMEM((1,), I32),
             DMA((2,)),
             DMA((7,)),
             DMA((8,)),
-            DMA((15,)),
+            DMA((16,)),
             DMA((16,)),
             DMA((16,)),
         ],
         compiler_params=params(collective_id=0, has_side_effects=True),
     )(
         weights,
-        count,
         members,
         pair_send,
+        count,
         values,
         cot,
         columns,
@@ -480,8 +501,8 @@
 ):
     index = pltpu.make_async_copy(columns_hbm, columns, index_sem)
     index.start()
-    for copy in tile_copies(tiles, buf, tile_sem, 5):
-        copy.start()
+    for first in range(AHEAD):
+        start_tiles(tiles, buf, tile_sem, first, 4)
 
     def project(i):
         part = z0[pl.ds(i * QUAD, QUAD), :]
@@ -493,7 +514,7 @@
     index.wait()
 
     def level(i):
-        wait_tiles(tiles, buf, tile_sem, i, 4)
+        next_tiles(tiles, buf, tile_sem, i, 4)
         parts = []
         for q in range(4):
             b = i * 4 + q
@@ -709,7 +730,7 @@
         [(h1_hbm, h1), (cot_hbm, cot), (gate_hbm, gate), (slope_hbm, slope)],
         load_sem.at[pl.ds(3, 4)],
     )
-    for copy in early + later:
+    for copy in early:
         copy.start()
     targets = [neighbour(me, n, -offset) for offset in OFFSETS]
     grads1[:H, :] = m1[...]
@@ -730,11 +751,13 @@
     for copy in back:
         copy.start()
     group.to_near()
+    for copy in early:
+        copy.wait()
+    for copy in later:
+        copy.start()
     cells[pl.ds(2 * (NC + HALO), 16), :] = jnp.zeros((16, H), F32)
     update_out[...] = jnp.zeros_like(update_out)
     named = lane_row(coarse_halo)
-    for copy in early:
-        copy.wait()
 
     def place(i):
         cells[pl.ds(i * 2 * QUAD, QUAD, stride=2), :] = z1[pl.ds(i * QUAD, QUAD), :].astype(F32)
@@ -907,24 +930,25 @@
     first = loads([(columns_hbm, columns), (grads_hbm, grads)], load_sem)
     for copy in first:
         copy.start()
-    for copy in tile_copies(tiles, buf, tile_sem, 8):
-        copy.start()
-    later = loads(
-        [(values_hbm, values), (halo_hbm, halo), (result_in, result)], load_sem.at[pl.ds(2, 3)]
-    )
-    for copy in later:
-        copy.start()
+    for ahead in range(AHEAD):
+        start_tiles(tiles, buf, tile_sem, ahead, 4)
     total[...] = jnp.zeros_like(total)
     for copy in first:
         copy.wait()
+    later = loads(
+        [(values_hbm, values), (halo_hbm, halo), (result_in, result)], load_sem.at[pl.ds(2, 3)]
+    )
 
     def level(i):
-        wait_tiles(tiles, buf, tile_sem, i, 4)
+        next_tiles(tiles, buf, tile_sem, i, 4)
         for q in range(4):
             b = i * 4 + q
             spread_row(buf, columns, jnp.transpose(grads[pl.ds(b * T, T), :]), b, total)
 
-    loop(6, level)
+    loop(2, level)
+    for copy in later:
+        copy.start()
+    loop(4, lambda i: level(i + 2))
     for copy in later:
         copy.wait()
     passed = pltpu.make_async_copy(result, result_out, store_sem.at[4])
@@ -972,12 +996,14 @@
     pieces,
     dm,
     low_hbm,
-    grad_out,
+    grad_hbm,
     total_out,
     arrived,
     rows,
     low,
+    grad_out,
     load_sem,
+    store_sem,
     send_sem,
     recv_sem,
     grads0,
@@ -1025,8 +1051,11 @@
     group.to_y()
     loop(5, lambda i: retract(i + 3))
     group.to_all()
+    stored = pltpu.make_async_copy(grad_out, grad_hbm, store_sem)
+    stored.start()
     group.wait()
     total_out[...] = group.total[...]
+    stored.wait()
 
 
 def fine_back(n, number, weights, fine_halo, m0, u0, pieces, dm, low):
@@ -1035,12 +1064,14 @@
         name="fine_back",
         out_shape=[shape((NF, H), BF16), shape((2 * H, H), F32)],
         in_specs=[VMEM] * 4 + [ANY] * 3,
-        out_specs=[VMEM] * 2,
+        out_specs=[ANY, VMEM],
         scratch_shapes=[
             pltpu.VMEM((HALO, H), BF16),
             pltpu.VMEM((NF, H), F32),
             pltpu.VMEM((NF, H), BF16),
+            pltpu.VMEM((NF, H), BF16),
             DMA((2,)),
+            DMA,
             DMA((4,)),
             DMA((4,)),
         ]

time: 117 us -> 115 us (0.983)
    pallas_call x1, Pallas kernels: 37.2 us -> 35.3 us  [forward(): pl.pallas_call(functools.partial(forward_kernel, n), name='forward', out_...]
    pallas_call x1, Pallas kernels: 29.8 us -> 31.2 us  [coarse_back(): pl.pallas_call(functools.partial(coarse_back_kernel, n), name='coarse_bac...]
where the time goes in v5:
time: 115 us
  Pallas kernels  114 us (99%)
  between operations  1.32 us (1%)
    pallas_call x1, Pallas kernels, forward(): pl.pallas_call(functools.partial(forward_kernel, n), name='forward', out_...  35.3 us
    pallas_call x1, Pallas kernels, coarse_back(): pl.pallas_call(functools.partial(coarse_back_kernel, n), name='coarse_bac...  31.2 us
    pallas_call x1, Pallas kernels, fine_back(): pl.pallas_call(functools.partial(fine_back_kernel, n), name='fine_back',...  23.1 us
    pallas_call x1, Pallas kernels, coarse_level(): pl.pallas_call(coarse_kernel, name='coarse_level', out_shape=[shape((NC,...  11.4 us
    pallas_call x1, Pallas kernels, fine_spread(): pl.pallas_call(fine_kernel, name='fine_spread', out_shape=[shape((NF, H),...  10.4 us
    pallas_call x1, Pallas kernels, finish(): pl.pallas_call(finish_kernel, name='finish', out_shape=[shape(grad.shape,...  2.42 us

profile of v5, /device:TPU:1, one launch (start us, length us, event | category | flops | bytes accessed | tf_op | source)
XLA Modules:
  0.0 115.2 jit_solution(12622665828336254857)
XLA Ops:
  1.3 35.3 %forward.1 = (bf16[4096,128]{1,0:T(8,128)(2,1)}, bf16[4096,128]{1,0:T(8,128)(2,1)}, bf16[4096,128]{1,0:T(8,128)(2,1)}, bf16[4,256,128]{2,1,0:T(8,128)(2,1)}, bf1...) custom-call(bf16[4,128,128]{2,1,0:T(8,128)(2,1)} %weights.7, ...), custom_call_target="tpu_custom_call" | custom-call | tf_op jit(solution)/shard_map/forward/pallas_call | solution.py:397
  36.6 11.4 %coarse_level.1 = (bf16[2560,128]{1,0:T(8,128)(2,1)}, f32[2560,128]{1,0:T(8,128)}, bf16[1024,128]{1,0:T(8,128)(2,1)}, f32[128,128]{1,0:T(8,128)}, f32[128,128]{1,0:T(8,128)}) custom-call(bf16[2560,128]{1,0:T(8,128)(2,1)} %get-tuple-element.29.z0, bf16[4,256,128]{2,1,0:T(8,128)(2,1)} %get-tuple-element.30.z0_halo, ...), custom_call_target="tpu_custom_call" | custom-call | tf_op jit(solution)/shard_map/coarse_level/pallas_call | solution.py:541
  48.0 31.2 %coarse_back.1 = (bf16[4096,128]{1,0:T(8,128)(2,1)}, bf16[4096,128]{1,0:T(8,128)(2,1)}, bf16[4096,128]{1,0:T(8,128)(2,1)}, f32[128,128]{1,0:T(8,128)}, f32[256,128]{1,0:T(8,128)}) custom-call(bf16[4,128,128]{2,1,0:T(8,128)(2,1)} %weights.7, s32[1,4,256]{2,1,0:T(4,128)} %coarse_halo.3, f32[128,128]{1,0:T(8,128)} %get-tuple-element.32.m1, ...), custom_call_target="tpu_custom_call" | custom-call | tf_op jit(solution)/shard_map/coarse_back/pallas_call | solution.py:853
  79.3 10.4 %fine_spread.1 = (f32[4096,128]{1,0:T(8,128)}, bf16[1024,128]{1,0:T(8,128)(2,1)}, f32[128,128]{1,0:T(8,128)}, bf16[4096,128]{1,0:T(8,128)(2,1)}) custom-call(bf16[4096,128]{1,0:T(8,128)(2,1)} %get-tuple-element.41.grads_hbm, bf16[4096,128]{1,0:T(8,128)(2,1)} %values_hbm.3, bf16[4,256,128]{2,1,0:T(8,128)(2,1)} %get-tuple-element.42.halo_hbm, ...), custom_call_target="tpu_custom_call" | custom-call | tf_op jit(solution)/shard_map/fine_spread/pallas_call | solution.py:962
  89.7 23.1 %fine_back.1 = (bf16[4096,128]{1,0:T(8,128)(2,1)}, f32[256,128]{1,0:T(8,128)}) custom-call(bf16[4,128,128]{2,1,0:T(8,128)(2,1)} %weights.7, s32[1,4,256]{2,1,0:T(4,128)} %fine_halo.3, f32[128,128]{1,0:T(8,128)} %get-tuple-element.45.m0, f32[128,128]{1,0:T(8,128)} %get-tuple-element.46.u0, bf16[1024,128]{1,0:T(8,128)(2,1)} %get-tuple-element.47.pieces, ...), custom_call_target="tpu_custom_call" | custom-call | tf_op jit(solution)/shard_map/fine_back/pallas_call | solution.py:1062
  112.8 2.4 %finish.1 = (bf16[4096,128]{1,0:T(8,128)(2,1)}, f32[4,128,128]{2,1,0:T(8,128)}) custom-call(bf16[4096,128]{1,0:T(8,128)(2,1)} %get-tuple-element.50.grad, f32[256,128]{1,0:T(8,128)} %get-tuple-element.51.fine, f32[256,128]{1,0:T(8,128)} %get-tuple-element.52.coarse), custom_call_target="tpu_custom_call" | custom-call | tf_op jit(solution)/shard_map/finish/pallas_call | solution.py:1090
